TPU v7x, 256 devices: a whole 4x4x8 slice. The times are simulated.
256 devices in a mesh: frame: 32 (over z_lo, x, core), head: 8 (over z_hi, y).
Axes of the slice: x: 4, y: 4, z: 8 (z_hi: 2, z_lo: 4; z = z_hi * 4 + z_lo), core: 2. Of those that a mesh axis runs over, the one named last changes fastest.
Arguments:
- queries: bfloat16 [32768, 5120], P(('frame', 'head')), may hold values from -6 to 6, as said below
- keys: bfloat16 [32768, 5120], P(('frame', 'head')), may hold values from -6 to 6, as said below
- values: bfloat16 [32768, 5120], P(('frame', 'head')), may hold values from -6 to 6
- q_gain: float32 [5120], replicated, may hold values from 0.5 to 2
- k_gain: float32 [5120], replicated, may hold values from 0.5 to 2
- block_ids: int32 [32, 8, 8], P('frame'), may hold values from 0 to 23, as said below
- counts: int32 [32, 8], P('frame'), may hold values from 1 to 8, as said below
- anchors: int32 [2], replicated, may hold values from 0 to 31, as said below
Outputs:
- attended: bfloat16 [32768, 5120], P(('frame', 'head'))
Inputs may be any that keep to these rules, and one draw needn't show every extreme that they name: `queries`: away from rare tokens, entries are of order one. `keys`: away from rare tokens, entries are of order one. `block_ids`: the 8 entries of one list are different; the first is the query block's own block b. `counts`: every view has a query block that uses all 8 listed blocks. `anchors`: the 2 anchor ids are different; one of them is the last view, 31.
All inputs are finite; a program needn't handle non-finite values.
Results may differ from a plain program's by a relative error of at most 0.012.
The roundings to bfloat16 on the way count: a program that leaves them out, or rounds other values in their place, can miss the bound.
Values may be sent and summed in bfloat16 or wider, within the bound.
No kernel may reach another device: no remote copies, remote signals or barrier semaphores. Data moves between devices by JAX's collectives and lax.ppermute only.
A program may use at most 128 MiB of HBM per device.

v0:
```python
import math

import jax
import jax.numpy as jnp
from jax import lax
from jax.sharding import PartitionSpec as P

HD = 128
BLOCK = 128


def spread(block, axis, owner):
    block = jnp.where(lax.axis_index(axis) == owner, block, jnp.zeros_like(block))
    return lax.psum(block, axis)


def normalize(rows, gain):
    wide = rows.astype(jnp.float32)
    square = jnp.mean(wide * wide, axis=-1, keepdims=True)
    return (wide * lax.rsqrt(square + 1e-06) * gain).astype(jnp.bfloat16)


def attend_view(q_heads, k_heads, v_heads, far_keys, far_values, block_ids, counts):
    view_len, local_width = q_heads.shape
    local_heads = local_width // HD
    blocks = view_len // BLOCK
    listed = block_ids.shape[2]
    group = math.gcd(blocks, max(1, 512 // BLOCK))
    steps = blocks // group
    key_blocks = jnp.concatenate([k_heads] + far_keys, axis=0).reshape(-1, BLOCK, local_heads, HD)
    value_blocks = jnp.concatenate([v_heads] + far_values, axis=0).reshape(
        -1, BLOCK, local_heads, HD
    )
    query_groups = q_heads.reshape(steps, group, BLOCK, local_heads, HD)
    id_groups = block_ids[0].reshape(steps, group, listed)
    count_groups = counts[0].reshape(steps, group)
    scale = 1.0 / math.sqrt(HD)
    slots = jnp.arange(listed, dtype=jnp.int32)

    def one_group(args):
        query_rows, id_lists, amount = args
        picked_k = key_blocks[id_lists]
        picked_v = value_blocks[id_lists]
        scores = (
            jnp.einsum(
                "gqhd,gkphd->ghqkp", query_rows, picked_k, preferred_element_type=jnp.float32
            )
            * scale
        )
        valid = (slots[None, :] < amount[:, None])[:, None, None, :, None]
        scores = jnp.where(valid, scores, -1e30)
        top = jnp.max(scores, axis=(3, 4), keepdims=True)
        expo = jnp.exp(scores - top)
        weights = (expo / jnp.sum(expo, axis=(3, 4), keepdims=True)).astype(jnp.bfloat16)
        mixed = jnp.einsum(
            "ghqkp,gkphd->gqhd", weights, picked_v, preferred_element_type=jnp.float32
        )
        return mixed.astype(jnp.bfloat16)

    result = lax.map(one_group, (query_groups, id_groups, count_groups))
    return result.reshape(view_len, local_width)


def shards(queries, keys, values, q_gain, k_gain, block_ids, counts, anchors):
    q_norm = normalize(queries, q_gain)
    k_norm = normalize(keys, k_gain)
    anchor_total = anchors.shape[0]
    far_keys = []
    far_values = []
    q_heads, k_heads, v_heads = (
        lax.all_to_all(q_norm, "head", split_axis=1, concat_axis=0, tiled=True),
        lax.all_to_all(k_norm, "head", split_axis=1, concat_axis=0, tiled=True),
        lax.all_to_all(values, "head", split_axis=1, concat_axis=0, tiled=True),
    )
    for anchor_slot in range(anchor_total):
        arrived = spread(jnp.stack([k_heads, v_heads]), "frame", anchors[anchor_slot])
        far_keys.append(arrived[0])
        far_values.append(arrived[1])
    mixed = attend_view(q_heads, k_heads, v_heads, far_keys, far_values, block_ids, counts)
    return lax.all_to_all(mixed, "head", split_axis=0, concat_axis=1, tiled=True)


def solution(mesh):
    placed = (
        P(("frame", "head"), None),
        P(("frame", "head"), None),
        P(("frame", "head"), None),
        P(),
        P(),
        P("frame", None, None),
        P("frame", None),
        P(),
    )
    return jax.shard_map(
        shards, mesh=mesh, in_specs=placed, out_specs=P(("frame", "head"), None), check_vma=False
    )
```

profile of v0, /device:TPU:32, one launch (start us, length us, event | category | flops | bytes accessed | tf_op | source)
XLA Modules:
  0.0 530.8 jit_solution(12391100707438150024)
XLA Ops:
  12.7 10.2 %all-to-all-start.1 = ((bf16[128,8,640]{2,0,1:T(8,128)(2,1)}), bf16[128,8,640]{2,0,1:T(8,128)(2,1)S(1)}, u32[]{:S(2)}, u32[]{:S(2)}) async-start(bf16[128,8,640]{2,0,1:T(8,128)(2,1)} %copy.47), calls=%async_computation.1 | async-start | bytes 2621440 | tf_op jit(solution)/shard_map/all_to_all | solution.py:72
  26.1 31.3 %all-to-all-done.1 = bf16[128,8,640]{2,0,1:T(8,128)(2,1)S(1)} async-done(((bf16[128,8,640]{2,0,1:T(8,128)(2,1)}), bf16[128,8,640]{2,0,1:T(8,128)(2,1)S(1)}, u32[]{:S(2)}, u32[]{:S(2)}) %all-to-all-start.1) | async-done | bytes 1310752 | tf_op jit(solution)/shard_map/all_to_all | solution.py:72
  57.4 4.6 all-to-all-start
  65.5 22.9 %all-to-all-done = bf16[128,8,640]{2,0,1:T(8,128)(2,1)S(1)} async-done(((bf16[128,8,640]{2,0,1:T(8,128)(2,1)}), bf16[128,8,640]{2,0,1:T(8,128)(2,1)S(1)}, u32[]{:S(2)}, u32[]{:S(2)}) %all-to-all-start) | async-done | bytes 1310752 | tf_op jit(solution)/shard_map/all_to_all | solution.py:73
  89.9 4.5 broadcast_select_fusion.1
  97.4 2.4 copy.51
  99.9 6.0 %all-to-all-start.2 = ((bf16[128,8,640]{0,2,1:T(8,128)(2,1)}), bf16[128,8,640]{0,2,1:T(8,128)(2,1)S(1)}, u32[]{:S(2)}, u32[]{:S(2)}) async-start(bf16[128,8,640]{0,2,1:T(8,128)(2,1)} %bitcast.126), calls=%async_computation.2 | async-start | bytes 2621440 | tf_op jit(solution)/shard_map/all_to_all | solution.py:71
  108.7 2.4 copy.50
  111.1 269.9 %all-reduce.3.cloned.1.call-done = (bf16[2,1024,640]{1,2,0:T(8,128)(2,1)}, bf16[2,1024,640]{1,2,0:T(8,128)(2,1)}) async-done(((bf16[2,1024,640]{1,2,0:T(8,128)(2,1)}, bf16[2,1024,640]{1,2,0:T(8,128)(2,1)}), (bf16[2,1024,640]{1,2,0:T(8,128)(2,1)}, bf16[2,1024,640]{1,2,0:T(8,128)(2,1)})) %all-reduce.3.cloned.1.call-update) | async-done | bytes 5242896 | tf_op jit(solution)/shard_map/psum | solution.py:14
  381.0 4.3 slice_bitcast_fusion
  385.6 3.0 copy.63
  388.6 7.7 %copy.55 = bf16[24,128,5,128]{3,2,1,0:T(8,128)(2,1)} copy(bf16[24,128,5,128]{1,0,3,2:T(8,128)(2,1)} %bitcast.120) | data formatting | bytes 7864320
  398.2 3.0 copy.62
  401.2 7.8 %copy.53 = bf16[24,128,5,128]{3,2,1,0:T(8,128)(2,1)} copy(bf16[24,128,5,128]{1,0,3,2:T(8,128)(2,1)} %bitcast.121) | data formatting | bytes 7864320
  409.0 73.8 %while.11 = (s32[]{:T(128)}, bf16[2,4,128,5,128]{2,4,3,1,0:T(8,128)(2,1)S(1)}, s32[2,4,8]{2,1,0:T(4,128)S(1)}, bf16[24,128,5,128]{3,2,1,0:T(8,128)(2,1)}, s32[2,...) while((s32[]{:T(128)}, ...), condition=%wide.region_7.8_spmd.clone, body=%wide.region_4.7_spmd.clone.sunk | while | flops 1373958272 | bytes 116723832 | solution.py:60
  409.3 7.8 %gather_fusion = bf16[32,128,5,128]{3,2,1,0:T(8,128)(2,1)} fusion(bf16[24,128,5,128]{3,2,1,0:T(8,128)(2,1)} %get-tuple-element.182, s32[1024]{0:T(1024)S(1)} %pad_clamp_fusion.2), kind=kCustom, calls=%fused_computation.1.clone.clone.1 | custom fusion | bytes 10485888 | tf_op jit(solution)/shard_map/while/body/eval_jaxpr/gather | solution.py:42
  417.1 4.9 copy.77
  427.7 7.9 %gather_fusion.1 = bf16[32,128,5,128]{3,2,1,0:T(8,128)(2,1)} fusion(bf16[24,128,5,128]{3,2,1,0:T(8,128)(2,1)} %get-tuple-element.179, s32[1024]{0:T(1024)S(1)} %pad_clamp_fusion.2), kind=kCustom, calls=%fused_computation.clone.clone.1 | custom fusion | bytes 10485888 | tf_op jit(solution)/shard_map/while/body/eval_jaxpr/gather | solution.py:43
  435.6 10.4 %fusion.45 = bf16[2,4,128,5,128]{2,4,3,1,0:T(8,128)(2,1)S(1)} fusion(bf16[2,4,128,5,128]{2,4,3,1,0:T(8,128)(2,1)S(1)} %get-tuple-element.169, s32[]{:T(128)} %get-tuple-element.168, f32[4,5,128,1024]{2,3,1,0} %copy-done, f32[4,5,128]{2,1,0:T(8,128)S(1)} %fusion.44, f32[4,5,128]{2,1,0:T(8,128)S(1)} %get-tuple-element.159, ...), kind=kOutput, calls=%fused_computation.14.clone.1 | convolution fusion | flops 684523520 | bytes 16417284 | tf_op jit(solution)/shard_map/while/body/eval_jaxpr/ghqkp,gkphd->gqhd/dot_general | solution.py:55
  446.1 7.8 %gather_fusion = bf16[32,128,5,128]{3,2,1,0:T(8,128)(2,1)} fusion(bf16[24,128,5,128]{3,2,1,0:T(8,128)(2,1)} %get-tuple-element.182, s32[1024]{0:T(1024)S(1)} %pad_clamp_fusion.2), kind=kCustom, calls=%fused_computation.1.clone.clone.1 | custom fusion | bytes 10485888 | tf_op jit(solution)/shard_map/while/body/eval_jaxpr/gather | solution.py:42
  453.9 4.9 copy.77
  464.5 7.9 %gather_fusion.1 = bf16[32,128,5,128]{3,2,1,0:T(8,128)(2,1)} fusion(bf16[24,128,5,128]{3,2,1,0:T(8,128)(2,1)} %get-tuple-element.179, s32[1024]{0:T(1024)S(1)} %pad_clamp_fusion.2), kind=kCustom, calls=%fused_computation.clone.clone.1 | custom fusion | bytes 10485888 | tf_op jit(solution)/shard_map/while/body/eval_jaxpr/gather | solution.py:43
  472.4 10.4 %fusion.45 = bf16[2,4,128,5,128]{2,4,3,1,0:T(8,128)(2,1)S(1)} fusion(bf16[2,4,128,5,128]{2,4,3,1,0:T(8,128)(2,1)S(1)} %get-tuple-element.169, s32[]{:T(128)} %get-tuple-element.168, f32[4,5,128,1024]{2,3,1,0} %copy-done, f32[4,5,128]{2,1,0:T(8,128)S(1)} %fusion.44, f32[4,5,128]{2,1,0:T(8,128)S(1)} %get-tuple-element.159, ...), kind=kOutput, calls=%fused_computation.14.clone.1 | convolution fusion | flops 684523520 | bytes 16417284 | tf_op jit(solution)/shard_map/while/body/eval_jaxpr/ghqkp,gkphd->gqhd/dot_general | solution.py:55
  483.5 38.1 %all_to_all.73 = bf16[8,128,640]{2,1,0:T(8,128)(2,1)S(1)} all-to-all(bf16[8,128,640]{2,1,0:T(8,128)(2,1)S(1)} %copy.56), channel_id=1, replica_groups=mesh['frame'=32,'head'=8] {'head'}, dimensions={0} | all-to-all | bytes 2621440 | tf_op jit(solution)/shard_map/all_to_all | solution.py:80
  (62 shorter events, 35.5 us)
Async XLA Ops:
  6.5 2.5 copy-start.6
  12.7 44.7 %all-to-all-start.1 = ((bf16[128,8,640]{2,0,1:T(8,128)(2,1)}), bf16[128,8,640]{2,0,1:T(8,128)(2,1)S(1)}, u32[]{:S(2)}, u32[]{:S(2)}) async-start(bf16[128,8,640]{2,0,1:T(8,128)(2,1)} %copy.47), calls=%async_computation.1 | async-start | bytes 2621440 | tf_op jit(solution)/shard_map/all_to_all | solution.py:72
  24.6 37.4 %copy-start.8 = (s32[2]{0:T(128)S(1)}, s32[2]{0:T(128)}, u32[]{:S(2)}) copy-start(s32[2]{0:T(128)} %param.17) | copy-start | bytes 28
  57.4 31.0 %all-to-all-start = ((bf16[128,8,640]{2,0,1:T(8,128)(2,1)}), bf16[128,8,640]{2,0,1:T(8,128)(2,1)S(1)}, u32[]{:S(2)}, u32[]{:S(2)}) async-start(bf16[128,8,640]{2,0,1:T(8,128)(2,1)} %copy.45), calls=%async_computation | async-start | bytes 2621440 | tf_op jit(solution)/shard_map/all_to_all | solution.py:73
  62.0 319.0 %all-reduce.3.cloned.1.call-start = ((), (), s32[]{:S(2)}) async-start(), calls=%async_computation.4 | async-start | bytes 10485760 | tf_op jit(solution)/shard_map/psum | solution.py:14
  88.4 6.0 %copy-start.1 = (bf16[128,8,640]{2,0,1:T(8,128)(2,1)}, bf16[128,8,640]{2,0,1:T(8,128)(2,1)S(1)}, u32[]{:S(2)}) copy-start(bf16[128,8,640]{2,0,1:T(8,128)(2,1)S(1)} %all-to-all-done) | copy-start | bytes 3932164
  94.3 1.3 copy-start.2
  94.3 1.7 copy-start.7
  97.4 9.0 %copy-start.9 = (s32[1,8]{1,0:T(1,128)S(1)}, s32[1,8]{1,0:T(1,128)}, u32[]{:S(2)}) copy-start(s32[1,8]{1,0:T(1,128)} %param.16) | copy-start | bytes 100
  99.9 309.1 %all-to-all-start.2 = ((bf16[128,8,640]{0,2,1:T(8,128)(2,1)}), bf16[128,8,640]{0,2,1:T(8,128)(2,1)S(1)}, u32[]{:S(2)}, u32[]{:S(2)}) async-start(bf16[128,8,640]{0,2,1:T(8,128)(2,1)} %bitcast.126), calls=%async_computation.2 | async-start | bytes 2621440 | tf_op jit(solution)/shard_map/all_to_all | solution.py:71
  381.0 4.3 copy-start.3
  401.2 7.8 %copy-start.4 = (bf16[2,4,128,5,128]{2,4,3,1,0:T(8,128)(2,1)S(1)}, bf16[2,4,128,5,128]{2,4,3,1,0:T(8,128)(2,1)}, u32[]{:S(2)}) copy-start(bf16[2,4,128,5,128]{2,4,3,1,0:T(8,128)(2,1)} %custom-call.4) | copy-start | bytes 3932164
  401.2 7.8 %copy-start.5 = (s32[1,8,8]{2,1,0:T(8,128)S(1)}, s32[1,8,8]{2,1,0:T(8,128)}, u32[]{:S(2)}) copy-start(s32[1,8,8]{2,1,0:T(8,128)} %param.15) | copy-start | bytes 772
  423.7 4.0 copy-start
  460.5 4.0 copy-start
Sparse Core Ops, SparseCore 0:
  94.5 286.4 all-reduce.2
where the time goes:
time: 535 us; the launch traced here: 531 us
  waiting for transfers between devices  324 us (61%)
  local copies, waits for them, and re-layouts  91.7 us (17%)
  blocking collectives  38.1 us (7%)
  matrix products  24 us (4%)
  starting transfers between devices  20.8 us (4%)
  other arithmetic  16.9 us (3%)
  between operations  14.8 us (3%)
    psum x1, waiting for transfers between devices, spread(): return lax.psum(block, axis)  270 us
    all_to_all x1, blocking collectives, shards(): lax.all_to_all(mixed, 'head', split_axis=0, concat_axis=1, tiled=True)  38.1 us
    all_to_all x1, waiting for transfers between devices, shards(): lax.all_to_all(k_norm, 'head', split_axis=1, concat_axis=0, tiled=True)  31.3 us
    unnamed x25, local copies, waits for them, and re-layouts  26.9 us
    gather x4, local copies, waits for them, and re-layouts, one_group(): picked_k = key_blocks[id_lists]  25.3 us
    all_to_all x1, waiting for transfers between devices, shards(): lax.all_to_all(values, 'head', split_axis=1, concat_axis=0, tiled=True)  22.9 us
    dot_general x2, matrix products, one_group(): jnp.einsum('ghqkp,gkphd->gqhd', weights, picked_v, preferred_element_type...  20.9 us
    gather x2, local copies, waits for them, and re-layouts, one_group(): picked_v = value_blocks[id_lists]  15.8 us
  transfers between devices with their start and end apart: 4, of which 3 were waited for; matrix products, arithmetic and copies ran while one was open for 8% of the time, Pallas kernels for 0%

commit v1 on v0

v1 whole, which is shorter than its diff:
```python
import functools
import math

import jax
import jax.numpy as jnp
from jax import lax
from jax.experimental import pallas as pl
from jax.experimental.pallas import tpu as pltpu
from jax.sharding import Mesh, PartitionSpec as P

HD = 128
BLOCK = 128
LISTED = 8
PLANES = 8
SHARE = 4
PER = SHARE + 1
TAIL = 16
SLOTS = 48
AXES = ("zl", "x", "c", "zh", "y")
PLANE = ("zl", "zh")
EVERY = ("zl", "zh", "y")
VMEM = 56 << 20
HALF = 32 << 20
ANY = pl.BlockSpec(memory_space=pl.ANY)
SMEM = pl.BlockSpec(memory_space=pltpu.SMEM)
F32 = jnp.float32
BF16 = jnp.bfloat16


def norm_kernel(q_ref, k_ref, v_ref, qg_ref, kg_ref, ids_ref, cnt_ref, q_out, kv_out, five_out):
    step, rows = pl.program_id(0), q_ref.shape[0]

    def normed(x_ref, g_ref):
        wide = x_ref[...].astype(F32)
        square = jnp.mean(wide * wide, axis=-1, keepdims=True)
        return (wide * lax.rsqrt(square + 1e-06) * g_ref[...]).astype(BF16)

    def place(wide, slot, put):
        for plane in range(PLANES):
            for lane in range(PER):
                at = (plane * PER + lane) * HD
                tile = wide[:, at : at + HD]
                if lane < SHARE:
                    put(plane * SHARE + lane, tile)
                else:
                    first = pl.multiple_of(slot * BLOCK + step * rows, 32)
                    five_out[plane, pl.ds(first, rows), :] = tile

    def put_q(head, tile):
        q_out[head] = tile

    def put_k(head, tile):
        kv_out[head, 0] = tile

    def put_v(head, tile):
        kv_out[head, 1] = tile

    place(normed(q_ref, qg_ref), 0, put_q)
    place(normed(k_ref, kg_ref), 1, put_k)
    place(v_ref[...], 2, put_v)

    @pl.when(step == 0)
    def _():
        row = lax.broadcasted_iota(jnp.int32, (TAIL, HD), 0)
        lane = lax.broadcasted_iota(jnp.int32, (TAIL, HD), 1)
        lists = jnp.zeros((TAIL, HD), jnp.int32)
        for b in range(ids_ref.shape[1]):
            for s in range(LISTED):
                lists = jnp.where((row == b) & (lane == s), ids_ref[0, b, s], lists)
            lists = jnp.where((row == b) & (lane == LISTED), cnt_ref[0, b], lists)
        for plane in range(PLANES):
            five_out[plane, 3 * BLOCK : 3 * BLOCK + TAIL, :] = lists.astype(F32).astype(BF16)


def norm_and_place(queries, keys, values, q_gain, k_gain, block_ids, counts):
    rows, width = queries.shape
    step = 32
    mains = PLANES * SHARE
    whole = pl.BlockSpec((step, width), lambda i: (i, 0))
    gain = pl.BlockSpec((1, width), lambda i: (0, 0))
    five_shape = (PLANES, 3 * rows + TAIL, HD)
    return pl.pallas_call(
        norm_kernel,
        grid=(rows // step,),
        in_specs=[whole, whole, whole, gain, gain, SMEM, SMEM],
        out_specs=[
            pl.BlockSpec((mains, step, HD), lambda i: (0, i, 0)),
            pl.BlockSpec((mains, 2, step, HD), lambda i: (0, 0, i, 0)),
            pl.BlockSpec(five_shape, lambda i: (0, 0, 0)),
        ],
        out_shape=[
            jax.ShapeDtypeStruct((mains, rows, HD), BF16),
            jax.ShapeDtypeStruct((mains, 2, rows, HD), BF16),
            jax.ShapeDtypeStruct(five_shape, BF16),
        ],
        compiler_params=pltpu.CompilerParams(vmem_limit_bytes=VMEM),
        name="norm_place",
    )(queries, keys, values, q_gain.reshape(1, -1), k_gain.reshape(1, -1), block_ids, counts)


def join_kernel(main_ref, five_ref, out_ref):
    for plane in range(PLANES):
        for lane in range(PER):
            at = (plane * PER + lane) * HD
            if lane < SHARE:
                out_ref[:, at : at + HD] = main_ref[plane * SHARE + lane]
            else:
                out_ref[:, at : at + HD] = five_ref[plane]


def join(main, five):
    rows = main.shape[1]
    step = 32
    width = PLANES * PER * HD
    return pl.pallas_call(
        join_kernel,
        grid=(rows // step,),
        in_specs=[
            pl.BlockSpec((main.shape[0], step, HD), lambda i: (0, i, 0)),
            pl.BlockSpec((PLANES, step, HD), lambda i: (0, i, 0)),
        ],
        out_specs=pl.BlockSpec((step, width), lambda i: (i, 0)),
        out_shape=jax.ShapeDtypeStruct((rows, width), BF16),
        compiler_params=pltpu.CompilerParams(vmem_limit_bytes=HALF),
        name="join_heads",
    )(main, five)


def attend_items(queries, picks, counts, kv, put):
    factor = math.log2(math.e) / math.sqrt(HD)
    ones = jnp.ones((LISTED * BLOCK, HD), BF16)
    scores, tops = [], []
    for query, pick, count in zip(queries, picks, counts):
        keys = jnp.concatenate([kv[p, 0:BLOCK, :] for p in pick], axis=0)
        raw = lax.dot_general(query(), keys, (((1,), (1,)), ((), ())), preferred_element_type=F32)
        parts = []
        for s in range(LISTED):
            bias = jnp.where(s < count, 0.0, -1e30).astype(F32)
            parts.append(raw[:, s * BLOCK : (s + 1) * BLOCK] * factor + bias)
        scores.append(parts)
        tops.append(jnp.max(functools.reduce(jnp.maximum, parts), axis=-1, keepdims=True))
    for i, pick in enumerate(picks):
        weights = jnp.concatenate([jnp.exp2(part - tops[i]).astype(BF16) for part in scores[i]], axis=1)
        values = jnp.concatenate([kv[p, BLOCK : 2 * BLOCK, :] for p in pick], axis=0)
        mixed = jnp.dot(weights, jnp.concatenate([values, ones], axis=1), preferred_element_type=F32)
        put(i, (mixed[:, :HD] / mixed[:, HD:]).astype(BF16))


def fetch(pairs, sems):
    copies = [pltpu.make_async_copy(src, dst, sems.at[i]) for i, (src, dst) in enumerate(pairs)]
    for copy in copies:
        copy.start()
    for copy in copies:
        copy.wait()


def main_kernel(pos_ref, lists_ref, q_ref, all_ref, own_ref, other_ref, out_ref, kv, sems):
    view, c = pl.program_id(0), pos_ref[2]

    @pl.when(view == 0)
    def _():
        pairs = [(all_ref, kv.at[pl.ds(0, 32)])]
        for a in range(2):
            pairs.append((own_ref.at[a], kv.at[pl.ds(32 + 8 * a + 4 * c, 4)]))
            pairs.append((other_ref.at[a], kv.at[pl.ds(32 + 8 * a + 4 * (1 - c), 4)]))
        fetch(pairs, sems)

    queries, picks, counts = [], [], []
    for b in range(8):
        queries.append(functools.partial(lambda b: q_ref[b], b))
        ids = [lists_ref[view, b, s] for s in range(LISTED)]
        picks.append([jnp.where(j < 8, view * 8 + j, 24 + j) for j in ids])
        counts.append(lists_ref[view, b, LISTED])

    def put(i, block):
        out_ref[i] = block

    attend_items(queries, picks, counts, kv, put)


def attend_main(pos, lists, q_all, kv_all, own, other):
    blocks = pl.BlockSpec((8, BLOCK, HD), lambda v: (v, 0, 0))
    return pl.pallas_call(
        main_kernel,
        grid=(4,),
        in_specs=[SMEM, SMEM, blocks, ANY, ANY, ANY],
        out_specs=blocks,
        out_shape=jax.ShapeDtypeStruct(q_all.shape, BF16),
        scratch_shapes=[pltpu.VMEM((SLOTS, 2 * BLOCK, HD), BF16), pltpu.SemaphoreType.DMA((5,))],
        compiler_params=pltpu.CompilerParams(vmem_limit_bytes=VMEM),
        cost_estimate=pl.CostEstimate(
            flops=32 * 4 * BLOCK * LISTED * BLOCK * HD,
            bytes_accessed=4 * SLOTS * BLOCK * HD,
            transcendentals=32 * BLOCK * LISTED * BLOCK,
        ),
        name="attend_main",
    )(pos, lists, q_all, kv_all, own, other)


def shared_kernel(pos_ref, lists_ref, q_ref, five_ref, pack_ref, *rest):
    y_own, y_anchor = rest[:3], rest[3:6]
    out_ref, kv, sems = rest[6:]
    c, y = pos_ref[2], pos_ref[3]
    pairs = [
        (five_ref.at[:, pl.ds(BLOCK, 2 * BLOCK)], kv.at[pl.ds(0, 8)]),
        (pack_ref, kv.at[pl.ds(8, 4)]),
    ]
    for d in (1, 2, 3):
        pairs.append((y_own[d - 1], kv.at[pl.ds(12 * d, 8)]))
        pairs.append((y_anchor[d - 1], kv.at[pl.ds(12 * d + 8, 4)]))
    fetch(pairs, sems)

    queries, picks, counts = [], [], []
    for i in range(PLANES):
        zl, zh = i // 2, i % 2
        queries.append(functools.partial(lambda i: q_ref[i], i))
        pick = []
        for s in range(LISTED):
            j = lists_ref[zl, 4 * zh + y, s]
            away = lax.rem(lax.rem(j, 4) - y + 4, 4)
            upper = lax.rem(j, 8) // 4
            far = 8 + 2 * lax.rem(upper + c, 2) + j // 8 - 1
            pick.append(12 * away + jnp.where(j < 8, 2 * zl + upper, far))
        picks.append(pick)
        counts.append(lists_ref[zl, 4 * zh + y, LISTED])

    def put(i, block):
        out_ref[i] = block

    attend_items(queries, picks, counts, kv, put)


def attend_shared(pos, lists, five, pack, y_own, y_anchor):
    blocks = pl.BlockSpec((PLANES, BLOCK, HD), lambda i: (0, 0, 0))
    return pl.pallas_call(
        shared_kernel,
        grid=(1,),
        in_specs=[SMEM, SMEM, blocks] + [ANY] * 8,
        out_specs=blocks,
        out_shape=jax.ShapeDtypeStruct((PLANES, BLOCK, HD), BF16),
        scratch_shapes=[pltpu.VMEM((SLOTS, 2 * BLOCK, HD), BF16), pltpu.SemaphoreType.DMA((8,))],
        compiler_params=pltpu.CompilerParams(vmem_limit_bytes=VMEM),
        cost_estimate=pl.CostEstimate(
            flops=8 * 4 * BLOCK * LISTED * BLOCK * HD,
            bytes_accessed=4 * SLOTS * BLOCK * HD,
            transcendentals=8 * BLOCK * LISTED * BLOCK,
        ),
        name="attend_shared",
    )(pos, lists, five, five, pack, *y_own, *y_anchor)


def shifted(x, axis, size, by):
    return lax.ppermute(x, axis, [((i + by) % size, i) for i in range(size)])


def core_half(by_zl, at_zl, at_c):
    c = lax.axis_index("c")
    mine = jnp.stack([lax.dynamic_index_in_dim(by_zl, at_zl[a], 0, keepdims=False) for a in range(2)], axis=1)
    kept = lax.dynamic_index_in_dim(mine, c, 0, keepdims=False)
    sent = lax.dynamic_index_in_dim(mine, 1 - c, 0, keepdims=False)
    here = (at_c == c).reshape((2,) + (1,) * (kept.ndim - 1))
    return jnp.where(here, kept, shifted(sent, "c", 2, 1))


def along_x(half):
    return [half] + [shifted(half, "x", 4, by) for by in (1, 2, 3)]


def both_halves(others, at_x):
    away = ((at_x - lax.axis_index("x")) % 4).reshape((2,) + (1,) * (others[0].ndim - 1))
    own = jnp.where(
        away < 2,
        jnp.where(away == 0, others[0], others[1]),
        jnp.where(away == 2, others[2], others[3]),
    )
    return own, shifted(own, "c", 2, 1)


def shards(queries, keys, values, q_gain, k_gain, block_ids, counts, anchors):
    at_zl, at_x, at_c = anchors // 8, (anchors // 2) % 4, anchors % 2
    pos = jnp.stack([lax.axis_index(axis) for axis in ("zl", "zh", "c", "y")])

    q_rows, kv_rows, five = norm_and_place(queries, keys, values, q_gain, k_gain, block_ids, counts)
    five = lax.all_to_all(five, PLANE, 0, 0, tiled=True)
    five, kv_rows, q_rows = lax.optimization_barrier((five, kv_rows, q_rows))
    kv_all = lax.all_to_all(kv_rows, EVERY, 0, 0, tiled=True).reshape(32, 2 * BLOCK, HD)

    lists = five.reshape(4, 2, -1, HD)[:, 0, 3 * BLOCK : 3 * BLOCK + 8, : LISTED + 1].astype(jnp.int32)
    kv_five = five[:, BLOCK : 3 * BLOCK]
    y_own = [shifted(kv_five, "y", 4, by) for by in (1, 2, 3)]
    half = core_half(kv_five.reshape(4, 2, 2 * BLOCK, HD), at_zl, at_c)
    pack = jnp.concatenate(both_halves(along_x(half), at_x), axis=0)
    kv_all, q_rows, pack, *y_own = lax.optimization_barrier((kv_all, q_rows, pack, *y_own))
    q_all = lax.all_to_all(q_rows, EVERY, 0, 0, tiled=True)

    others = along_x(core_half(kv_all.reshape(4, 2, 4, 2 * BLOCK, HD), at_zl, at_c))
    y_anchor = [shifted(pack, "y", 4, by) for by in (1, 2, 3)]
    shared = attend_shared(pos, lists, five, pack, y_own, y_anchor)
    shared, q_all, *others = lax.optimization_barrier((shared, q_all, *others))
    shared = lax.all_to_all(shared, PLANE, 0, 0, tiled=True)
    own, other = both_halves(others, at_x)
    mixed = attend_main(pos, lists, q_all, kv_all, own, other)
    main = lax.all_to_all(mixed, EVERY, 0, 0, tiled=True)
    return join(main, shared)


def solution(mesh):
    fine = Mesh(mesh.devices.reshape(4, 4, 2, 2, 4), AXES)
    tokens = P(AXES, None)
    frame = ("zl", "x", "c")
    placed = (tokens, tokens, tokens, P(), P(), P(frame, None, None), P(frame, None), P())
    return jax.shard_map(shards, mesh=fine, in_specs=placed, out_specs=tokens, check_vma=False)
```

time: 535 us -> 201 us (0.38)
  waiting for transfers between devices: 324 us -> 54.5 us
  local copies, waits for them, and re-layouts: 91.7 us -> 3.98 us
  blocking collectives: 38.1 us -> 68.9 us
  matrix products: 24 us -> 0 us
  Pallas kernels: 0 us -> 22.8 us
  starting transfers between devices: 20.8 us -> 43 us
  other arithmetic: 16.9 us -> 1.87 us
  between operations: 14.8 us -> 4.35 us
    psum x1 -> x0, waiting for transfers between devices: 270 us -> none  [spread(): return lax.psum(block, axis)]
    ppermute x0 -> x16, waiting for transfers between devices: none -> 54.4 us  [shifted(): return lax.ppermute(x, axis, [((i + by) % size, i) for i in range(size)])]
    all_to_all x3, waiting for transfers between devices: 54.2 us -> 0.06 us  [the longest x1 0.06 us: shards(): shared = lax.all_to_all(shared, PLANE, 0, 0, tiled=True)]
    gather x6 -> x0, local copies, waits for them, and re-layouts: 41.1 us -> none  [the longest x4 25.3 us: one_group(): picked_k = key_blocks[id_lists]]
    all_to_all x1 -> x2, blocking collectives: 38.1 us -> 68.9 us  [the longest x1 38.1 us: shards(): main = lax.all_to_all(mixed, EVERY, 0, 0, tiled=True)]
    unnamed x25 -> x22, local copies, waits for them, and re-layouts: 26.9 us -> 3.15 us
    pallas_call x0 -> x4, Pallas kernels: none -> 22.8 us  [the longest x1 9.84 us: attend_main(): pl.pallas_call(main_kernel, grid=(4,), in_specs=[SMEM, SMEM, blocks, ANY,...]
    dot_general x2 -> x0, matrix products: 20.9 us -> none  [one_group(): jnp.einsum('ghqkp,gkphd->gqhd', weights, picked_v, preferred_element_type...]
  transfers between devices with their start and end apart: 4 -> 19, of which waited for: 3 -> 9; matrix products, arithmetic and copies ran while one was open for 8% -> 1% of each run, Pallas kernels for 0% -> 8%
where the time goes in v1:
time: 201 us; the launch traced here: 199 us
  blocking collectives  68.9 us (34%)
  waiting for transfers between devices  54.5 us (27%)
  starting transfers between devices  43 us (21%)
  Pallas kernels  22.8 us (11%)
  between operations  4.35 us (2%)
  local copies, waits for them, and re-layouts  3.98 us (2%)
    ppermute x16, waiting for transfers between devices, shifted(): return lax.ppermute(x, axis, [((i + by) % size, i) for i in range(size)])  54.4 us
    all_to_all x1, blocking collectives, shards(): main = lax.all_to_all(mixed, EVERY, 0, 0, tiled=True)  38.1 us
    all_to_all x1, blocking collectives, shards(): five = lax.all_to_all(five, PLANE, 0, 0, tiled=True)  30.9 us
    ppermute x16, starting transfers between devices, shifted(): return lax.ppermute(x, axis, [((i + by) % size, i) for i in range(size)])  19.4 us
    pallas_call x1, Pallas kernels, attend_main(): pl.pallas_call(main_kernel, grid=(4,), in_specs=[SMEM, SMEM, blocks, ANY,...  9.84 us
    all_to_all x1, starting transfers between devices, shards(): q_all = lax.all_to_all(q_rows, EVERY, 0, 0, tiled=True)  8.98 us
    all_to_all x1, starting transfers between devices, shards(): shared = lax.all_to_all(shared, PLANE, 0, 0, tiled=True)  8.39 us
    all_to_all x1, starting transfers between devices, shards(): lax.all_to_all(kv_rows, EVERY, 0, 0, tiled=True).reshape(32, 2 * BLOCK, HD)  6.27 us
  transfers between devices with their start and end apart: 19, of which 9 were waited for; matrix products, arithmetic and copies ran while one was open for 1% of the time, Pallas kernels for 8%

profile of v1, /device:TPU:32, one launch (start us, length us, event | category | flops | bytes accessed | tf_op | source)
XLA Modules:
  0.0 199.4 jit_solution(1694372816833164499)
XLA Ops:
  0.0 5.5 %norm_place.1 = (bf16[32,128,128]{2,1,0:T(8,128)(2,1)}, bf16[32,2,128,128]{3,2,1,0:T(8,128)(2,1)}, bf16[8,400,128]{2,1,0:T(8,128)(2,1)}) custom-call(bf16[128,5120]{1,0:T(8,128)(2,1)} %q_ref.1, bf16[128,5120]{1,0:T(8,128)(2,1)} %k_ref.1, bf16[128,5120]{1,0:T(8,128)(2,1)} %v_ref.1, f32[1,5120]{1,0:T(1,128)} %bitcast.43, f32[1,5120]{1,0:T(1,128)} %bitcast.44, ...), custom_call_target="tpu_custom_call" | custom-call | tf_op jit(solution)/shard_map/norm_place/pallas_call | solution.py:82
  5.5 30.9 %all_to_all.25.q_ref.five_ref = bf16[8,400,128]{2,1,0:T(8,128)(2,1)S(1)} all-to-all(bf16[8,400,128]{2,1,0:T(8,128)(2,1)} %get-tuple-element.23), channel_id=1, replica_groups=mesh['zl'=4,'x'=4,'c'=2,'zh'=2,'y'=4] {'zl','zh'}, dimensions={0} | all-to-all | bytes 1638400 | tf_op jit(solution)/shard_map/all_to_all | solution.py:284
  36.4 6.3 %all-to-all-start.1 = ((bf16[32,2,128,128]{3,2,1,0:T(8,128)(2,1)}), bf16[32,2,128,128]{3,2,1,0:T(8,128)(2,1)S(1)}, u32[]{:S(2)}, u32[]{:S(2)}) async-start(bf16[32,2,128,128]{3,2,1,0:T(8,128)(2,1)} %get-tuple-element.27), calls=%async_computation.1 | async-start | bytes 4194304 | tf_op jit(solution)/shard_map/all_to_all | solution.py:286
  47.7 1.3 collective-permute-done
  49.1 3.1 %collective-permute-start.2 = (bf16[2,256,128]{2,1,0:T(8,128)(2,1)S(1)}, bf16[2,256,128]{2,1,0:T(8,128)(2,1)S(1)}, u32[]{:S(2)}, u32[]{:S(2)}) collective-permute-start(bf16[2,256,128]{2,1,0:T(8,128)(2,1)S(1)} %fusion.9), channel_id=1, source_target_pairs={{32,0},{48,16},{0,32},{16,48},{33,1},{49,17},{1,33},{17,49},{34,2}... | collective-permute-start | bytes 393224 | tf_op jit(solution)/shard_map/ppermute | solution.py:253
  52.2 2.7 %collective-permute-start.5 = (bf16[8,256,128]{2,1,0:T(8,128)(2,1)S(1)}, bf16[8,256,128]{2,1,0:T(8,128)(2,1)S(1)}, u32[]{:S(2)}, u32[]{:S(2)}) collective-permute-start(bf16[8,256,128]{2,1,0:T(8,128)(2,1)S(1)} %slice.15), channel_id=1, source_target_pairs={{1,0},{2,1},{3,2},{0,3},{5,4},{6,5},{7,6},{4,7},{9,8},{10,9},{11,1... | collective-permute-start | bytes 1572872 | tf_op jit(solution)/shard_map/ppermute | solution.py:253
  57.2 2.6 %collective-permute-start.1 = (bf16[2,256,128]{2,1,0:T(8,128)(2,1)S(1)}, bf16[2,256,128]{2,1,0:T(8,128)(2,1)S(1)}, u32[]{:S(2)}, u32[]{:S(2)}) collective-permute-start(bf16[2,256,128]{2,1,0:T(8,128)(2,1)S(1)} %fusion.9), channel_id=1, source_target_pairs={{16,0},{32,16},{48,32},{0,48},{17,1},{33,17},{49,33},{1,49},{18,2}... | collective-permute-start | bytes 393224 | tf_op jit(solution)/shard_map/ppermute | solution.py:253
  59.9 2.9 %collective-permute-done.3 = bf16[2,256,128]{2,1,0:T(8,128)(2,1)S(1)} collective-permute-done((bf16[2,256,128]{2,1,0:T(8,128)(2,1)S(1)}, bf16[2,256,128]{2,1,0:T(8,128)(2,1)S(1)}, u32[]{:S(2)}, u32[]{:S(2)}) %collective-permute-start.3) | collective-permute-done | bytes 131104 | tf_op jit(solution)/shard_map/ppermute | solution.py:253
  63.0 1.3 collective-permute-done.4
  64.4 25.8 %collective-permute-done.5.rest_0_ = bf16[8,256,128]{2,1,0:T(8,128)(2,1)S(1)} collective-permute-done((bf16[8,256,128]{2,1,0:T(8,128)(2,1)S(1)}, bf16[8,256,128]{2,1,0:T(8,128)(2,1)S(1)}, u32[]{:S(2)}, u32[]{:S(2)}) %collective-permute-start.5) | collective-permute-done | bytes 524320 | tf_op jit(solution)/shard_map/ppermute | solution.py:253
  91.8 4.1 %collective-permute-done.7.rest_2_ = bf16[8,256,128]{2,1,0:T(8,128)(2,1)} collective-permute-done((bf16[8,256,128]{2,1,0:T(8,128)(2,1)S(1)}, bf16[8,256,128]{2,1,0:T(8,128)(2,1)}, u32[]{:S(2)}, u32[]{:S(2)}) %collective-permute-start.7) | collective-permute-done | bytes 524320 | tf_op jit(solution)/shard_map/ppermute | solution.py:253
  95.9 9.0 %all-to-all-start.2 = ((bf16[32,128,128]{2,1,0:T(8,128)(2,1)}), bf16[32,128,128]{2,1,0:T(8,128)(2,1)}, u32[]{:S(2)}, u32[]{:S(2)}) async-start(bf16[32,128,128]{2,1,0:T(8,128)(2,1)} %get-tuple-element.33), calls=%async_computation.2 | async-start | bytes 2097152 | tf_op jit(solution)/shard_map/all_to_all | solution.py:294
  105.2 2.8 %collective-permute-start.8 = (bf16[4,256,128]{2,1,0:T(8,128)(2,1)S(1)}, bf16[4,256,128]{2,1,0:T(8,128)(2,1)S(1)}, u32[]{:S(2)}, u32[]{:S(2)}) collective-permute-start(bf16[4,256,128]{2,1,0:T(8,128)(2,1)S(1)} %pad_maximum_fusion.pack_ref), channel_id=1, source_target_pairs={{1,0},{2,1},{3,2},{0,3},{5,4},{6,5},{7,6},{4,7},{9,8},{10,9},{11,1... | collective-permute-start | bytes 786440 | tf_op jit(solution)/shard_map/ppermute | solution.py:253
  108.1 2.1 %collective-permute-start.12 = (bf16[2,4,256,128]{3,2,1,0:T(8,128)(2,1)S(1)}, bf16[2,4,256,128]{3,2,1,0:T(8,128)(2,1)S(1)}, u32[]{:S(2)}, u32[]{:S(2)}) collective-permute-start(bf16[2,4,256,128]{3,2,1,0:T(8,128)(2,1)S(1)} %fusion.4), channel_id=1, source_target_pairs={{16,0},{32,16},{48,32},{0,48},{17,1},{33,17},{49,33},{1,49},{18,2}... | collective-permute-start | bytes 1572872 | tf_op jit(solution)/shard_map/ppermute | solution.py:253
  110.2 1.1 collective-permute-start.13
  111.5 2.1 %collective-permute-start.9 = (bf16[4,256,128]{2,1,0:T(8,128)(2,1)S(1)}, bf16[4,256,128]{2,1,0:T(8,128)(2,1)S(1)}, u32[]{:S(2)}, u32[]{:S(2)}) collective-permute-start(bf16[4,256,128]{2,1,0:T(8,128)(2,1)S(1)} %pad_maximum_fusion.pack_ref), channel_id=1, source_target_pairs={{2,0},{3,1},{0,2},{1,3},{6,4},{7,5},{4,6},{5,7},{10,8},{11,9},{8,1... | collective-permute-start | bytes 786440 | tf_op jit(solution)/shard_map/ppermute | solution.py:253
  113.6 8.5 %collective-permute-done.8.rest_3_ = bf16[4,256,128]{2,1,0:T(8,128)(2,1)S(1)} collective-permute-done((bf16[4,256,128]{2,1,0:T(8,128)(2,1)S(1)}, bf16[4,256,128]{2,1,0:T(8,128)(2,1)S(1)}, u32[]{:S(2)}, u32[]{:S(2)}) %collective-permute-start.8) | collective-permute-done | bytes 262176 | tf_op jit(solution)/shard_map/ppermute | solution.py:253
  123.4 3.6 %collective-permute-done.9.rest_4_ = bf16[4,256,128]{2,1,0:T(8,128)(2,1)S(1)} collective-permute-done((bf16[4,256,128]{2,1,0:T(8,128)(2,1)S(1)}, bf16[4,256,128]{2,1,0:T(8,128)(2,1)S(1)}, u32[]{:S(2)}, u32[]{:S(2)}) %collective-permute-start.9) | collective-permute-done | bytes 262176 | tf_op jit(solution)/shard_map/ppermute | solution.py:253
  127.0 6.8 %collective-permute-done.10.rest_5_ = bf16[4,256,128]{2,1,0:T(8,128)(2,1)S(1)} collective-permute-done((bf16[4,256,128]{2,1,0:T(8,128)(2,1)S(1)}, bf16[4,256,128]{2,1,0:T(8,128)(2,1)S(1)}, u32[]{:S(2)}, u32[]{:S(2)}) %collective-permute-start.10) | collective-permute-done | bytes 262176 | tf_op jit(solution)/shard_map/ppermute | solution.py:253
  134.5 5.6 %attend_shared.1 = bf16[8,128,128]{2,1,0:T(8,128)(2,1)} custom-call(s32[4]{0:T(128)} %pad_add_fusion.pos_ref, s32[4,8,9]{2,1,0:T(8,128)} %fusion.10.lists_ref, bf16[8,400,128]{2,1,0:T(8,128)(2,1)} %copy-done, bf16[8,400,128]{2,1,0:T(8,128)(2,1)} %copy-done, bf16[4,256,128]{2,1,0:T(8,128)(2,1)} %copy-done.2, bf16[8,256,128]{2,1,0:T(8,128)(2,1)} %copy-done.3, ...), custom_call_target="tpu_custom_call" | custom-call | flops 536870912 | bytes 3145728 | tf_op jit(solution)/shard_map/attend_shared/pallas_call | solution.py:235
  140.5 8.4 %all-to-all-start.4 = ((bf16[8,128,128]{2,1,0:T(8,128)(2,1)}), bf16[8,128,128]{2,1,0:T(8,128)(2,1)S(1)}, u32[]{:S(2)}, u32[]{:S(2)}) async-start(bf16[8,128,128]{2,1,0:T(8,128)(2,1)} %attend_shared.1), calls=%async_computation.4 | async-start | bytes 524288 | tf_op jit(solution)/shard_map/all_to_all | solution.py:300
  149.7 9.8 %attend_main.1 = bf16[32,128,128]{2,1,0:T(8,128)(2,1)} custom-call(s32[4]{0:T(128)} %pad_add_fusion.pos_ref, s32[4,8,9]{2,1,0:T(8,128)} %fusion.10.lists_ref, bf16[32,128,128]{2,1,0:T(8,128)(2,1)} %all-to-all-done.2.q_ref, bf16[32,256,128]{2,1,0:T(8,128)(2,1)} %bitcast.41, bf16[2,4,256,128]{3,2,1,0:T(8,128)(2,1)} %copy-done.5, ...), custom_call_target="tpu_custom_call" | custom-call | flops 2147483648 | bytes 3145728 | tf_op jit(solution)/shard_map/attend_main/pallas_call | solution.py:183
  159.6 38.1 %all_to_all.26.main_ref = bf16[32,128,128]{2,1,0:T(8,128)(2,1)S(1)} all-to-all(bf16[32,128,128]{2,1,0:T(8,128)(2,1)} %attend_main.1), channel_id=1, replica_groups=mesh['zl'=4,'x'=4,'c'=2,'zh'=2,'y'=4] {'zl','zh','y'}, dimensions={0} | all-to-all | bytes 2097152 | tf_op jit(solution)/shard_map/all_to_all | solution.py:303
  197.6 1.8 join_heads.1
  (58 shorter events, 8.8 us)
Async XLA Ops:
  36.4 86.4 %copy-start = (bf16[8,400,128]{2,1,0:T(8,128)(2,1)}, bf16[8,400,128]{2,1,0:T(8,128)(2,1)S(1)}, u32[]{:S(2)}) copy-start(bf16[8,400,128]{2,1,0:T(8,128)(2,1)S(1)} %all_to_all.25.q_ref.five_ref) | copy-start | bytes 2457604
  36.4 59.5 %all-to-all-start.1 = ((bf16[32,2,128,128]{3,2,1,0:T(8,128)(2,1)}), bf16[32,2,128,128]{3,2,1,0:T(8,128)(2,1)S(1)}, u32[]{:S(2)}, u32[]{:S(2)}) async-start(bf16[32,2,128,128]{3,2,1,0:T(8,128)(2,1)} %get-tuple-element.27), calls=%async_computation.1 | async-start | bytes 4194304 | tf_op jit(solution)/shard_map/all_to_all | solution.py:286
  47.6 1.4 collective-permute-start
  49.1 8.1 %collective-permute-start.2 = (bf16[2,256,128]{2,1,0:T(8,128)(2,1)S(1)}, bf16[2,256,128]{2,1,0:T(8,128)(2,1)S(1)}, u32[]{:S(2)}, u32[]{:S(2)}) collective-permute-start(bf16[2,256,128]{2,1,0:T(8,128)(2,1)S(1)} %fusion.9), channel_id=1, source_target_pairs={{32,0},{48,16},{0,32},{16,48},{33,1},{49,17},{1,33},{17,49},{34,2}... | collective-permute-start | bytes 393224 | tf_op jit(solution)/shard_map/ppermute | solution.py:253
  52.2 37.9 %collective-permute-start.5 = (bf16[8,256,128]{2,1,0:T(8,128)(2,1)S(1)}, bf16[8,256,128]{2,1,0:T(8,128)(2,1)S(1)}, u32[]{:S(2)}, u32[]{:S(2)}) collective-permute-start(bf16[8,256,128]{2,1,0:T(8,128)(2,1)S(1)} %slice.15), channel_id=1, source_target_pairs={{1,0},{2,1},{3,2},{0,3},{5,4},{6,5},{7,6},{4,7},{9,8},{10,9},{11,1... | collective-permute-start | bytes 1572872 | tf_op jit(solution)/shard_map/ppermute | solution.py:253
  54.9 35.3 %collective-permute-start.6 = (bf16[8,256,128]{2,1,0:T(8,128)(2,1)S(1)}, bf16[8,256,128]{2,1,0:T(8,128)(2,1)S(1)}, u32[]{:S(2)}, u32[]{:S(2)}) collective-permute-start(bf16[8,256,128]{2,1,0:T(8,128)(2,1)S(1)} %slice.15), channel_id=1, source_target_pairs={{2,0},{3,1},{0,2},{1,3},{6,4},{7,5},{4,6},{5,7},{10,8},{11,9},{8,1... | collective-permute-start | bytes 1572872 | tf_op jit(solution)/shard_map/ppermute | solution.py:253
  55.8 40.1 %collective-permute-start.7 = (bf16[8,256,128]{2,1,0:T(8,128)(2,1)S(1)}, bf16[8,256,128]{2,1,0:T(8,128)(2,1)}, u32[]{:S(2)}, u32[]{:S(2)}) collective-permute-start(bf16[8,256,128]{2,1,0:T(8,128)(2,1)S(1)} %slice.15), channel_id=1, source_target_pairs={{3,0},{0,1},{1,2},{2,3},{7,4},{4,5},{5,6},{6,7},{11,8},{8,9},{9,10... | collective-permute-start | bytes 1572872 | tf_op jit(solution)/shard_map/ppermute | solution.py:253
  56.6 6.2 %collective-permute-start.3 = (bf16[2,256,128]{2,1,0:T(8,128)(2,1)S(1)}, bf16[2,256,128]{2,1,0:T(8,128)(2,1)S(1)}, u32[]{:S(2)}, u32[]{:S(2)}) collective-permute-start(bf16[2,256,128]{2,1,0:T(8,128)(2,1)S(1)} %fusion.9), channel_id=1, source_target_pairs={{48,0},{0,16},{16,32},{32,48},{49,1},{1,17},{17,33},{33,49},{50,2}... | collective-permute-start | bytes 393224 | tf_op jit(solution)/shard_map/ppermute | solution.py:253
  57.2 5.6 %collective-permute-start.1 = (bf16[2,256,128]{2,1,0:T(8,128)(2,1)S(1)}, bf16[2,256,128]{2,1,0:T(8,128)(2,1)S(1)}, u32[]{:S(2)}, u32[]{:S(2)}) collective-permute-start(bf16[2,256,128]{2,1,0:T(8,128)(2,1)S(1)} %fusion.9), channel_id=1, source_target_pairs={{16,0},{32,16},{48,32},{0,48},{17,1},{33,17},{49,33},{1,49},{18,2}... | collective-permute-start | bytes 393224 | tf_op jit(solution)/shard_map/ppermute | solution.py:253
  62.9 1.4 collective-permute-start.4
  64.4 57.7 %copy-start.2 = (bf16[4,256,128]{2,1,0:T(8,128)(2,1)}, bf16[4,256,128]{2,1,0:T(8,128)(2,1)S(1)}, u32[]{:S(2)}) copy-start(bf16[4,256,128]{2,1,0:T(8,128)(2,1)S(1)} %pad_maximum_fusion.pack_ref) | copy-start | bytes 786436
  95.9 9.1 %copy-start.1 = (bf16[32,2,128,128]{3,2,1,0:T(8,128)(2,1)}, bf16[32,2,128,128]{3,2,1,0:T(8,128)(2,1)S(1)}, u32[]{:S(2)}) copy-start(bf16[32,2,128,128]{3,2,1,0:T(8,128)(2,1)S(1)} %all-to-all-done.1) | copy-start | bytes 6291460
  95.9 44.3 %all-to-all-start.2 = ((bf16[32,128,128]{2,1,0:T(8,128)(2,1)}), bf16[32,128,128]{2,1,0:T(8,128)(2,1)}, u32[]{:S(2)}, u32[]{:S(2)}) async-start(bf16[32,128,128]{2,1,0:T(8,128)(2,1)} %get-tuple-element.33), calls=%async_computation.2 | async-start | bytes 2097152 | tf_op jit(solution)/shard_map/all_to_all | solution.py:294
  105.1 2.9 %collective-permute-start.11 = (bf16[2,4,256,128]{3,2,1,0:T(8,128)(2,1)S(1)}, bf16[2,4,256,128]{3,2,1,0:T(8,128)(2,1)S(1)}, u32[]{:S(2)}, u32[]{:S(2)}) collective-permute-start(bf16[2,4,256,128]{3,2,1,0:T(8,128)(2,1)S(1)} %fusion.1), channel_id=1, source_target_pairs={{8,0},{0,8},{9,1},{1,9},{10,2},{2,10},{11,3},{3,11},{12,4},{4,12},... | collective-permute-start | bytes 1572872 | tf_op jit(solution)/shard_map/ppermute | solution.py:253
  105.2 16.9 %collective-permute-start.8 = (bf16[4,256,128]{2,1,0:T(8,128)(2,1)S(1)}, bf16[4,256,128]{2,1,0:T(8,128)(2,1)S(1)}, u32[]{:S(2)}, u32[]{:S(2)}) collective-permute-start(bf16[4,256,128]{2,1,0:T(8,128)(2,1)S(1)} %pad_maximum_fusion.pack_ref), channel_id=1, source_target_pairs={{1,0},{2,1},{3,2},{0,3},{5,4},{6,5},{7,6},{4,7},{9,8},{10,9},{11,1... | collective-permute-start | bytes 786440 | tf_op jit(solution)/shard_map/ppermute | solution.py:253
  108.1 32.1 %collective-permute-start.12 = (bf16[2,4,256,128]{3,2,1,0:T(8,128)(2,1)S(1)}, bf16[2,4,256,128]{3,2,1,0:T(8,128)(2,1)S(1)}, u32[]{:S(2)}, u32[]{:S(2)}) collective-permute-start(bf16[2,4,256,128]{3,2,1,0:T(8,128)(2,1)S(1)} %fusion.4), channel_id=1, source_target_pairs={{16,0},{32,16},{48,32},{0,48},{17,1},{33,17},{49,33},{1,49},{18,2}... | collective-permute-start | bytes 1572872 | tf_op jit(solution)/shard_map/ppermute | solution.py:253
  110.2 30.0 %collective-permute-start.13 = (bf16[2,4,256,128]{3,2,1,0:T(8,128)(2,1)S(1)}, bf16[2,4,256,128]{3,2,1,0:T(8,128)(2,1)S(1)}, u32[]{:S(2)}, u32[]{:S(2)}) collective-permute-start(bf16[2,4,256,128]{3,2,1,0:T(8,128)(2,1)S(1)} %fusion.4), channel_id=1, source_target_pairs={{32,0},{48,16},{0,32},{16,48},{33,1},{49,17},{1,33},{17,49},{34,2}... | collective-permute-start | bytes 1572872 | tf_op jit(solution)/shard_map/ppermute | solution.py:253
  111.3 28.9 %collective-permute-start.14 = (bf16[2,4,256,128]{3,2,1,0:T(8,128)(2,1)S(1)}, bf16[2,4,256,128]{3,2,1,0:T(8,128)(2,1)S(1)}, u32[]{:S(2)}, u32[]{:S(2)}) collective-permute-start(bf16[2,4,256,128]{3,2,1,0:T(8,128)(2,1)S(1)} %fusion.4), channel_id=1, source_target_pairs={{48,0},{0,16},{16,32},{32,48},{49,1},{1,17},{17,33},{33,49},{50,2}... | collective-permute-start | bytes 1572872 | tf_op jit(solution)/shard_map/ppermute | solution.py:253
  111.5 15.5 %collective-permute-start.9 = (bf16[4,256,128]{2,1,0:T(8,128)(2,1)S(1)}, bf16[4,256,128]{2,1,0:T(8,128)(2,1)S(1)}, u32[]{:S(2)}, u32[]{:S(2)}) collective-permute-start(bf16[4,256,128]{2,1,0:T(8,128)(2,1)S(1)} %pad_maximum_fusion.pack_ref), channel_id=1, source_target_pairs={{2,0},{3,1},{0,2},{1,3},{6,4},{7,5},{4,6},{5,7},{10,8},{11,9},{8,1... | collective-permute-start | bytes 786440 | tf_op jit(solution)/shard_map/ppermute | solution.py:253
  122.1 11.7 %copy-start.6 = (bf16[4,256,128]{2,1,0:T(8,128)(2,1)}, bf16[4,256,128]{2,1,0:T(8,128)(2,1)S(1)}, u32[]{:S(2)}) copy-start(bf16[4,256,128]{2,1,0:T(8,128)(2,1)S(1)} %collective-permute-done.8.rest_3_) | copy-start | bytes 786436
  122.1 11.7 %collective-permute-start.10 = (bf16[4,256,128]{2,1,0:T(8,128)(2,1)S(1)}, bf16[4,256,128]{2,1,0:T(8,128)(2,1)S(1)}, u32[]{:S(2)}, u32[]{:S(2)}) collective-permute-start(bf16[4,256,128]{2,1,0:T(8,128)(2,1)S(1)} %pad_maximum_fusion.pack_ref), channel_id=1, source_target_pairs={{3,0},{0,1},{1,2},{2,3},{7,4},{4,5},{5,6},{6,7},{11,8},{8,9},{9,10... | collective-permute-start | bytes 786440 | tf_op jit(solution)/shard_map/ppermute | solution.py:253
  140.4 8.5 %copy-start.5 = (bf16[2,4,256,128]{3,2,1,0:T(8,128)(2,1)}, bf16[2,4,256,128]{3,2,1,0:T(8,128)(2,1)S(1)}, u32[]{:S(2)}) copy-start(bf16[2,4,256,128]{3,2,1,0:T(8,128)(2,1)S(1)} %select_select_fusion.own_ref) | copy-start | bytes 1572868
  140.4 8.5 %collective-permute-start.15 = (bf16[2,4,256,128]{3,2,1,0:T(8,128)(2,1)S(1)}, bf16[2,4,256,128]{3,2,1,0:T(8,128)(2,1)S(1)}, u32[]{:S(2)}, u32[]{:S(2)}) collective-permute-start(bf16[2,4,256,128]{3,2,1,0:T(8,128)(2,1)S(1)} %select_select_fusion.own_ref), channel_id=1, source_target_pairs={{8,0},{0,8},{9,1},{1,9},{10,2},{2,10},{11,3},{3,11},{12,4},{4,12},... | collective-permute-start | bytes 1572872 | tf_op jit(solution)/shard_map/ppermute | solution.py:253
  140.5 19.1 %all-to-all-start.4 = ((bf16[8,128,128]{2,1,0:T(8,128)(2,1)}), bf16[8,128,128]{2,1,0:T(8,128)(2,1)S(1)}, u32[]{:S(2)}, u32[]{:S(2)}) async-start(bf16[8,128,128]{2,1,0:T(8,128)(2,1)} %attend_shared.1), calls=%async_computation.4 | async-start | bytes 524288 | tf_op jit(solution)/shard_map/all_to_all | solution.py:300
  (6 other events, 16.2 us)

commit v2 on v1

--- a/solution.py
+++ b/solution.py
@@ -27,75 +27,86 @@
 BF16 = jnp.bfloat16
 
 
-def norm_kernel(q_ref, k_ref, v_ref, qg_ref, kg_ref, ids_ref, cnt_ref, q_out, kv_out, five_out):
+def inverse(x_ref):
+    wide = x_ref[...].astype(F32)
+    square = jnp.mean(wide * wide, axis=-1, keepdims=True)
+    return lax.rsqrt(square + 1e-06)
+
+
+def normed(x_ref, scale, g_ref, head):
+    at = slice(head * HD, (head + 1) * HD)
+    return (x_ref[:, at].astype(F32) * scale * g_ref[:, at]).astype(BF16)
+
+
+def shared_rows_kernel(q_ref, k_ref, v_ref, qg_ref, kg_ref, ids_ref, cnt_ref, out_ref):
     step, rows = pl.program_id(0), q_ref.shape[0]
-
-    def normed(x_ref, g_ref):
-        wide = x_ref[...].astype(F32)
-        square = jnp.mean(wide * wide, axis=-1, keepdims=True)
-        return (wide * lax.rsqrt(square + 1e-06) * g_ref[...]).astype(BF16)
-
-    def place(wide, slot, put):
-        for plane in range(PLANES):
-            for lane in range(PER):
-                at = (plane * PER + lane) * HD
-                tile = wide[:, at : at + HD]
-                if lane < SHARE:
-                    put(plane * SHARE + lane, tile)
-                else:
-                    first = pl.multiple_of(slot * BLOCK + step * rows, 32)
-                    five_out[plane, pl.ds(first, rows), :] = tile
-
-    def put_q(head, tile):
-        q_out[head] = tile
-
-    def put_k(head, tile):
-        kv_out[head, 0] = tile
-
-    def put_v(head, tile):
-        kv_out[head, 1] = tile
-
-    place(normed(q_ref, qg_ref), 0, put_q)
-    place(normed(k_ref, kg_ref), 1, put_k)
-    place(v_ref[...], 2, put_v)
+    q_scale, k_scale = inverse(q_ref), inverse(k_ref)
+    for plane in range(PLANES):
+        head = plane * PER + SHARE
+        tiles = (
+            normed(q_ref, q_scale, qg_ref, head),
+            normed(k_ref, k_scale, kg_ref, head),
+            v_ref[:, head * HD : (head + 1) * HD],
+        )
+        for slot, tile in enumerate(tiles):
+            out_ref[plane, pl.ds(pl.multiple_of(slot * BLOCK + step * rows, 32), rows), :] = tile
 
     @pl.when(step == 0)
     def _():
         row = lax.broadcasted_iota(jnp.int32, (TAIL, HD), 0)
         lane = lax.broadcasted_iota(jnp.int32, (TAIL, HD), 1)
         lists = jnp.zeros((TAIL, HD), jnp.int32)
-        for b in range(ids_ref.shape[1]):
+        for b in range(8):
             for s in range(LISTED):
                 lists = jnp.where((row == b) & (lane == s), ids_ref[0, b, s], lists)
             lists = jnp.where((row == b) & (lane == LISTED), cnt_ref[0, b], lists)
         for plane in range(PLANES):
-            five_out[plane, 3 * BLOCK : 3 * BLOCK + TAIL, :] = lists.astype(F32).astype(BF16)
-
-
-def norm_and_place(queries, keys, values, q_gain, k_gain, block_ids, counts):
+            out_ref[plane, 3 * BLOCK : 3 * BLOCK + TAIL, :] = lists.astype(F32).astype(BF16)
+
+
+def own_rows_kernel(q_ref, k_ref, v_ref, qg_ref, kg_ref, q_out, kv_out):
+    q_scale, k_scale = inverse(q_ref), inverse(k_ref)
+    for plane in range(PLANES):
+        for lane in range(SHARE):
+            to, head = plane * SHARE + lane, plane * PER + lane
+            q_out[to] = normed(q_ref, q_scale, qg_ref, head)
+            kv_out[to, 0] = normed(k_ref, k_scale, kg_ref, head)
+            kv_out[to, 1] = v_ref[:, head * HD : (head + 1) * HD]
+
+
+def placed(queries, keys, values, q_gain, k_gain, block_ids, counts):
     rows, width = queries.shape
     step = 32
-    mains = PLANES * SHARE
+    heads = PLANES * SHARE
     whole = pl.BlockSpec((step, width), lambda i: (i, 0))
     gain = pl.BlockSpec((1, width), lambda i: (0, 0))
-    five_shape = (PLANES, 3 * rows + TAIL, HD)
-    return pl.pallas_call(
-        norm_kernel,
+    shared = (PLANES, 3 * rows + TAIL, HD)
+    inputs = (queries, keys, values, q_gain.reshape(1, -1), k_gain.reshape(1, -1))
+    five = pl.pallas_call(
+        shared_rows_kernel,
         grid=(rows // step,),
         in_specs=[whole, whole, whole, gain, gain, SMEM, SMEM],
+        out_specs=pl.BlockSpec(shared, lambda i: (0, 0, 0)),
+        out_shape=jax.ShapeDtypeStruct(shared, BF16),
+        compiler_params=pltpu.CompilerParams(vmem_limit_bytes=VMEM),
+        name="shared_rows",
+    )(*inputs, block_ids, counts)
+    q_rows, kv_rows = pl.pallas_call(
+        own_rows_kernel,
+        grid=(rows // step,),
+        in_specs=[whole, whole, whole, gain, gain],
         out_specs=[
-            pl.BlockSpec((mains, step, HD), lambda i: (0, i, 0)),
-            pl.BlockSpec((mains, 2, step, HD), lambda i: (0, 0, i, 0)),
-            pl.BlockSpec(five_shape, lambda i: (0, 0, 0)),
+            pl.BlockSpec((heads, step, HD), lambda i: (0, i, 0)),
+            pl.BlockSpec((heads, 2, step, HD), lambda i: (0, 0, i, 0)),
         ],
         out_shape=[
-            jax.ShapeDtypeStruct((mains, rows, HD), BF16),
-            jax.ShapeDtypeStruct((mains, 2, rows, HD), BF16),
-            jax.ShapeDtypeStruct(five_shape, BF16),
+            jax.ShapeDtypeStruct((heads, rows, HD), BF16),
+            jax.ShapeDtypeStruct((heads, 2, rows, HD), BF16),
         ],
         compiler_params=pltpu.CompilerParams(vmem_limit_bytes=VMEM),
-        name="norm_place",
-    )(queries, keys, values, q_gain.reshape(1, -1), k_gain.reshape(1, -1), block_ids, counts)
+        name="own_rows",
+    )(*inputs)
+    return five, q_rows, kv_rows
 
 
 def join_kernel(main_ref, five_ref, out_ref):
@@ -197,56 +208,58 @@
     )(pos, lists, q_all, kv_all, own, other)
 
 
-def shared_kernel(pos_ref, lists_ref, q_ref, five_ref, pack_ref, *rest):
-    y_own, y_anchor = rest[:3], rest[3:6]
-    out_ref, kv, sems = rest[6:]
+def shared_kernel(pos_ref, lists_ref, five_ref, *rest):
+    got, near_ref, far_ref = rest[:3], rest[3], rest[4]
+    outs, q, kv, sems = rest[5:9], rest[9], rest[10], rest[11]
     c, y = pos_ref[2], pos_ref[3]
-    pairs = [
-        (five_ref.at[:, pl.ds(BLOCK, 2 * BLOCK)], kv.at[pl.ds(0, 8)]),
-        (pack_ref, kv.at[pl.ds(8, 4)]),
-    ]
-    for d in (1, 2, 3):
-        pairs.append((y_own[d - 1], kv.at[pl.ds(12 * d, 8)]))
-        pairs.append((y_anchor[d - 1], kv.at[pl.ds(12 * d + 8, 4)]))
+    pairs = [(near_ref, kv.at[pl.ds(8, 8)]), (far_ref, kv.at[pl.ds(16, 8)])]
+    for d in range(4):
+        mine = five_ref.at[pl.ds(2 * y, 2)] if d == 0 else got[d - 1]
+        pairs.append((mine.at[:, pl.ds(0, BLOCK)], q.at[pl.ds(2 * d, 2)]))
+        pairs.append((mine.at[:, pl.ds(BLOCK, 2 * BLOCK)], kv.at[pl.ds(2 * d, 2)]))
     fetch(pairs, sems)
 
     queries, picks, counts = [], [], []
-    for i in range(PLANES):
-        zl, zh = i // 2, i % 2
-        queries.append(functools.partial(lambda i: q_ref[i], i))
+    for i in range(8):
+        row = 4 * (i % 2) + lax.rem(y + i // 2, 4)
+        queries.append(functools.partial(lambda i: q[i], i))
         pick = []
         for s in range(LISTED):
-            j = lists_ref[zl, 4 * zh + y, s]
+            j = lists_ref[y, row, s]
             away = lax.rem(lax.rem(j, 4) - y + 4, 4)
             upper = lax.rem(j, 8) // 4
-            far = 8 + 2 * lax.rem(upper + c, 2) + j // 8 - 1
-            pick.append(12 * away + jnp.where(j < 8, 2 * zl + upper, far))
+            far = 8 + 8 * lax.rem(upper + c, 2) + 2 * away + j // 8 - 1
+            pick.append(jnp.where(j < 8, 2 * away + upper, far))
         picks.append(pick)
-        counts.append(lists_ref[zl, 4 * zh + y, LISTED])
+        counts.append(lists_ref[y, row, LISTED])
 
     def put(i, block):
-        out_ref[i] = block
+        outs[i // 2][i % 2] = block
 
     attend_items(queries, picks, counts, kv, put)
 
 
-def attend_shared(pos, lists, five, pack, y_own, y_anchor):
-    blocks = pl.BlockSpec((PLANES, BLOCK, HD), lambda i: (0, 0, 0))
+def attend_shared(pos, lists, five, got, near, far):
+    blocks = pl.BlockSpec((2, BLOCK, HD), lambda i: (0, 0, 0))
     return pl.pallas_call(
         shared_kernel,
         grid=(1,),
-        in_specs=[SMEM, SMEM, blocks] + [ANY] * 8,
-        out_specs=blocks,
-        out_shape=jax.ShapeDtypeStruct((PLANES, BLOCK, HD), BF16),
-        scratch_shapes=[pltpu.VMEM((SLOTS, 2 * BLOCK, HD), BF16), pltpu.SemaphoreType.DMA((8,))],
+        in_specs=[SMEM, SMEM] + [ANY] * 6,
+        out_specs=[blocks] * SHARE,
+        out_shape=[jax.ShapeDtypeStruct((2, BLOCK, HD), BF16)] * SHARE,
+        scratch_shapes=[
+            pltpu.VMEM((8, BLOCK, HD), BF16),
+            pltpu.VMEM((24, 2 * BLOCK, HD), BF16),
+            pltpu.SemaphoreType.DMA((10,)),
+        ],
         compiler_params=pltpu.CompilerParams(vmem_limit_bytes=VMEM),
         cost_estimate=pl.CostEstimate(
             flops=8 * 4 * BLOCK * LISTED * BLOCK * HD,
-            bytes_accessed=4 * SLOTS * BLOCK * HD,
+            bytes_accessed=4 * 24 * BLOCK * HD,
             transcendentals=8 * BLOCK * LISTED * BLOCK,
         ),
         name="attend_shared",
-    )(pos, lists, five, five, pack, *y_own, *y_anchor)
+    )(pos, lists, five, *got, near, far)
 
 
 def shifted(x, axis, size, by):
@@ -266,42 +279,52 @@
     return [half] + [shifted(half, "x", 4, by) for by in (1, 2, 3)]
 
 
-def both_halves(others, at_x):
+def true_half(others, at_x):
     away = ((at_x - lax.axis_index("x")) % 4).reshape((2,) + (1,) * (others[0].ndim - 1))
-    own = jnp.where(
+    return jnp.where(
         away < 2,
         jnp.where(away == 0, others[0], others[1]),
         jnp.where(away == 2, others[2], others[3]),
     )
-    return own, shifted(own, "c", 2, 1)
 
 
 def shards(queries, keys, values, q_gain, k_gain, block_ids, counts, anchors):
     at_zl, at_x, at_c = anchors // 8, (anchors // 2) % 4, anchors % 2
     pos = jnp.stack([lax.axis_index(axis) for axis in ("zl", "zh", "c", "y")])
 
-    q_rows, kv_rows, five = norm_and_place(queries, keys, values, q_gain, k_gain, block_ids, counts)
+    five, q_rows, kv_rows = placed(queries, keys, values, q_gain, k_gain, block_ids, counts)
     five = lax.all_to_all(five, PLANE, 0, 0, tiled=True)
     five, kv_rows, q_rows = lax.optimization_barrier((five, kv_rows, q_rows))
     kv_all = lax.all_to_all(kv_rows, EVERY, 0, 0, tiled=True).reshape(32, 2 * BLOCK, HD)
 
-    lists = five.reshape(4, 2, -1, HD)[:, 0, 3 * BLOCK : 3 * BLOCK + 8, : LISTED + 1].astype(jnp.int32)
-    kv_five = five[:, BLOCK : 3 * BLOCK]
-    y_own = [shifted(kv_five, "y", 4, by) for by in (1, 2, 3)]
-    half = core_half(kv_five.reshape(4, 2, 2 * BLOCK, HD), at_zl, at_c)
-    pack = jnp.concatenate(both_halves(along_x(half), at_x), axis=0)
-    kv_all, q_rows, pack, *y_own = lax.optimization_barrier((kv_all, q_rows, pack, *y_own))
+    y = lax.axis_index("y")
+    by_view = five.reshape(4, 2, -1, HD)
+    lists = by_view[:, 0, 3 * BLOCK : 3 * BLOCK + 8, : LISTED + 1].astype(jnp.int32)
+    half = core_half(by_view[:, :, BLOCK : 3 * BLOCK], at_zl, at_c)
+    half = true_half(along_x(half), at_x)
+    got = []
+    for by in (1, 2, 3):
+        view = lax.dynamic_index_in_dim(by_view[:, :, : 3 * BLOCK], (y - by) % 4, 0, keepdims=False)
+        got.append(shifted(view, "y", 4, by))
+    near = jnp.concatenate([half] + [shifted(half, "y", 4, by) for by in (1, 2, 3)], axis=0)
+    far = shifted(near, "c", 2, 1)
+    kv_all, q_rows, near, far, *got = lax.optimization_barrier((kv_all, q_rows, near, far, *got))
     q_all = lax.all_to_all(q_rows, EVERY, 0, 0, tiled=True)
 
-    others = along_x(core_half(kv_all.reshape(4, 2, 4, 2 * BLOCK, HD), at_zl, at_c))
-    y_anchor = [shifted(pack, "y", 4, by) for by in (1, 2, 3)]
-    shared = attend_shared(pos, lists, five, pack, y_own, y_anchor)
+    half = core_half(kv_all.reshape(4, 2, 4, 2 * BLOCK, HD), at_zl, at_c)
+    half, near = lax.optimization_barrier((half, near))
+    others = along_x(half)
+    parts = attend_shared(pos, lists, five, got, near, far)
+    back = jnp.stack([parts[0]] + [shifted(parts[d], "y", 4, -d) for d in (3, 2, 1)])
+    shared = lax.dynamic_slice_in_dim(jnp.concatenate([back, back]), 4 - y, 4, 0).reshape(PLANES, BLOCK, HD)
+    shared, q_all = lax.optimization_barrier((shared, q_all))
+    home = lax.all_to_all(shared, PLANE, 0, 0, tiled=True)
     shared, q_all, *others = lax.optimization_barrier((shared, q_all, *others))
-    shared = lax.all_to_all(shared, PLANE, 0, 0, tiled=True)
-    own, other = both_halves(others, at_x)
+    own = true_half(others, at_x)
+    other = shifted(own, "c", 2, 1)
     mixed = attend_main(pos, lists, q_all, kv_all, own, other)
     main = lax.all_to_all(mixed, EVERY, 0, 0, tiled=True)
-    return join(main, shared)
+    return join(main, home)
 
 
 def solution(mesh):

time: 201 us -> 198 us (0.985)
  blocking collectives: 68.9 us -> 39 us
  waiting for transfers between devices: 54.5 us -> 64.8 us
  starting transfers between devices: 43 us -> 52.3 us
  Pallas kernels: 22.8 us -> 25.9 us
  other arithmetic: 1.87 us -> 4.67 us
  local copies, waits for them, and re-layouts: 3.98 us -> 6.25 us
    all_to_all x1 -> x0, blocking collectives: 30.9 us -> none  [shards(): five = lax.all_to_all(five, PLANE, 0, 0, tiled=True)]
    all_to_all x1 -> x2, waiting for transfers between devices: 0.06 us -> 16 us  [the longest x1 15.9 us: shards(): five = lax.all_to_all(five, PLANE, 0, 0, tiled=True)]
    ppermute x16 -> x19, waiting for transfers between devices: 54.4 us -> 46.4 us  [shifted(): return lax.ppermute(x, axis, [((i + by) % size, i) for i in range(size)])]
    all_to_all x1 -> x2, starting transfers between devices: 8.39 us -> 15.1 us  [the longest x1 8.57 us: shards(): five = lax.all_to_all(five, PLANE, 0, 0, tiled=True)]
    pallas_call x2 -> x3, Pallas kernels: 11.2 us -> 14.3 us  [the longest x1 5.2 us: attend_shared(): pl.pallas_call(shared_kernel, grid=(1,), in_specs=[SMEM, SMEM] + [ANY] *...]
    all_to_all x1, waiting for transfers between devices: 0.01 us -> 2.48 us  [shards(): q_all = lax.all_to_all(q_rows, EVERY, 0, 0, tiled=True)]
    unnamed x22 -> x29, local copies, waits for them, and re-layouts: 3.15 us -> 4.66 us
    ppermute x16 -> x19, starting transfers between devices: 19.4 us -> 20.4 us  [shifted(): return lax.ppermute(x, axis, [((i + by) % size, i) for i in range(size)])]
  transfers between devices with their start and end apart: 19 -> 23, of which waited for: 9 -> 15; matrix products, arithmetic and copies ran while one was open for 1% -> 3% of each run, Pallas kernels for 8% -> 10%
where the time goes in v2:
time: 198 us; the launch traced here: 197 us
  waiting for transfers between devices  64.8 us (33%)
  starting transfers between devices  52.3 us (26%)
  blocking collectives  39 us (20%)
  Pallas kernels  25.9 us (13%)
  local copies, waits for them, and re-layouts  6.25 us (3%)
  other arithmetic  4.67 us (2%)
  between operations  4.03 us (2%)
    ppermute x19, waiting for transfers between devices, shifted(): return lax.ppermute(x, axis, [((i + by) % size, i) for i in range(size)])  46.4 us
    all_to_all x1, blocking collectives, shards(): main = lax.all_to_all(mixed, EVERY, 0, 0, tiled=True)  39 us
    ppermute x19, starting transfers between devices, shifted(): return lax.ppermute(x, axis, [((i + by) % size, i) for i in range(size)])  20.4 us
    all_to_all x1, waiting for transfers between devices, shards(): five = lax.all_to_all(five, PLANE, 0, 0, tiled=True)  15.9 us
    pallas_call x1, Pallas kernels, attend_main(): pl.pallas_call(main_kernel, grid=(4,), in_specs=[SMEM, SMEM, blocks, ANY,...  9.83 us
    all_to_all x1, starting transfers between devices, shards(): q_all = lax.all_to_all(q_rows, EVERY, 0, 0, tiled=True)  9.05 us
    all_to_all x1, starting transfers between devices, shards(): five = lax.all_to_all(five, PLANE, 0, 0, tiled=True)  8.57 us
    all_to_all x1, starting transfers between devices, shards(): lax.all_to_all(kv_rows, EVERY, 0, 0, tiled=True).reshape(32, 2 * BLOCK, HD)  7.87 us
  transfers between devices with their start and end apart: 23, of which 15 were waited for; matrix products, arithmetic and copies ran while one was open for 3% of the time, Pallas kernels for 10%

profile of v2, /device:TPU:32, one launch (start us, length us, event | category | flops | bytes accessed | tf_op | source)
XLA Modules:
  0.0 197.0 jit_solution(5432422864332034069)
XLA Ops:
  0.0 4.2 %shared_rows.1 = bf16[8,400,128]{2,1,0:T(8,128)(2,1)} custom-call(bf16[128,5120]{1,0:T(8,128)(2,1)} %q_ref.3, bf16[128,5120]{1,0:T(8,128)(2,1)} %k_ref.3, bf16[128,5120]{1,0:T(8,128)(2,1)} %v_ref.3, f32[1,5120]{1,0:T(1,128)} %bitcast.62, f32[1,5120]{1,0:T(1,128)} %bitcast.64, s32[1,8,8]{2,1,0:T(8,128)} %ids_ref.1, s32[1,8]{1,0:T(1,128)} %cnt_ref.1), custom_call_target="tpu_custom_call" | custom-call | tf_op jit(solution)/shard_map/shared_rows/pallas_call | solution.py:85
  4.2 8.6 %all-to-all-start = ((bf16[8,400,128]{2,1,0:T(8,128)(2,1)}), bf16[8,400,128]{2,1,0:T(8,128)(2,1)S(1)}, u32[]{:S(2)}, u32[]{:S(2)}) async-start(bf16[8,400,128]{2,1,0:T(8,128)(2,1)} %shared_rows.1), calls=%async_computation | async-start | bytes 1638400 | tf_op jit(solution)/shard_map/all_to_all | solution.py:296
  12.8 4.9 %own_rows.1 = (bf16[32,128,128]{2,1,0:T(8,128)(2,1)}, bf16[32,2,128,128]{3,2,1,0:T(8,128)(2,1)}) custom-call(bf16[128,5120]{1,0:T(8,128)(2,1)} %q_ref.3, bf16[128,5120]{1,0:T(8,128)(2,1)} %k_ref.3, bf16[128,5120]{1,0:T(8,128)(2,1)} %v_ref.3, f32[1,5120]{1,0:T(1,128)} %bitcast.63, f32[1,5120]{1,0:T(1,128)} %bitcast.65), custom_call_target="tpu_custom_call" | custom-call | tf_op jit(solution)/shard_map/own_rows/pallas_call | solution.py:94
  17.7 15.9 %all-to-all-done.five_ref = bf16[8,400,128]{2,1,0:T(8,128)(2,1)S(1)} async-done(((bf16[8,400,128]{2,1,0:T(8,128)(2,1)}), bf16[8,400,128]{2,1,0:T(8,128)(2,1)S(1)}, u32[]{:S(2)}, u32[]{:S(2)}) %all-to-all-start) | async-done | bytes 819232 | tf_op jit(solution)/shard_map/all_to_all | solution.py:296
  33.5 7.9 %all-to-all-start.1 = ((bf16[32,2,128,128]{3,2,1,0:T(8,128)(2,1)}), bf16[32,2,128,128]{3,2,1,0:T(8,128)(2,1)S(1)}, u32[]{:S(2)}, u32[]{:S(2)}) async-start(bf16[32,2,128,128]{3,2,1,0:T(8,128)(2,1)} %get-tuple-element.33), calls=%async_computation.1 | async-start | bytes 4194304 | tf_op jit(solution)/shard_map/all_to_all | solution.py:298
  47.4 2.8 %collective-permute-start.1 = (bf16[2,256,128]{2,1,0:T(8,128)(2,1)S(1)}, bf16[2,256,128]{2,1,0:T(8,128)(2,1)S(1)}, u32[]{:S(2)}, u32[]{:S(2)}) collective-permute-start(bf16[2,256,128]{2,1,0:T(8,128)(2,1)S(1)} %fusion.9), channel_id=1, source_target_pairs={{16,0},{32,16},{48,32},{0,48},{17,1},{33,17},{49,33},{1,49},{18,2}... | collective-permute-start | bytes 393224 | tf_op jit(solution)/shard_map/ppermute | solution.py:266
  51.9 4.2 %collective-permute-done.1 = bf16[2,256,128]{2,1,0:T(8,128)(2,1)S(1)} collective-permute-done((bf16[2,256,128]{2,1,0:T(8,128)(2,1)S(1)}, bf16[2,256,128]{2,1,0:T(8,128)(2,1)S(1)}, u32[]{:S(2)}, u32[]{:S(2)}) %collective-permute-start.1) | collective-permute-done | bytes 131104 | tf_op jit(solution)/shard_map/ppermute | solution.py:266
  56.2 2.0 %collective-permute-done.2 = bf16[2,256,128]{2,1,0:T(8,128)(2,1)S(1)} collective-permute-done((bf16[2,256,128]{2,1,0:T(8,128)(2,1)S(1)}, bf16[2,256,128]{2,1,0:T(8,128)(2,1)S(1)}, u32[]{:S(2)}, u32[]{:S(2)}) %collective-permute-start.2) | collective-permute-done | bytes 131104 | tf_op jit(solution)/shard_map/ppermute | solution.py:266
  59.9 2.8 %collective-permute-start.4 = (bf16[2,256,128]{2,1,0:T(8,128)(2,1)S(1)}, bf16[2,256,128]{2,1,0:T(8,128)(2,1)S(1)}, u32[]{:S(2)}, u32[]{:S(2)}) collective-permute-start(bf16[2,256,128]{2,1,0:T(8,128)(2,1)S(1)} %select_select_fusion.1), channel_id=1, source_target_pairs={{1,0},{2,1},{3,2},{0,3},{5,4},{6,5},{7,6},{4,7},{9,8},{10,9},{11,1... | collective-permute-start | bytes 393224 | tf_op jit(solution)/shard_map/ppermute | solution.py:266
  64.4 13.2 %collective-permute-done.4 = bf16[2,256,128]{2,1,0:T(8,128)(2,1)S(1)} collective-permute-done((bf16[2,256,128]{2,1,0:T(8,128)(2,1)S(1)}, bf16[2,256,128]{2,1,0:T(8,128)(2,1)S(1)}, u32[]{:S(2)}, u32[]{:S(2)}) %collective-permute-start.4) | collective-permute-done | bytes 131104 | tf_op jit(solution)/shard_map/ppermute | solution.py:266
  80.1 3.2 %collective-permute-start.8 = (bf16[2,384,128]{2,1,0:T(8,128)(2,1)S(1)}, bf16[2,384,128]{2,1,0:T(8,128)(2,1)S(1)}, u32[]{:S(2)}, u32[]{:S(2)}) collective-permute-start(bf16[2,384,128]{2,1,0:T(8,128)(2,1)S(1)} %get-tuple-element.61), channel_id=1, source_target_pairs={{1,0},{2,1},{3,2},{0,3},{5,4},{6,5},{7,6},{4,7},{9,8},{10,9},{11,1... | collective-permute-start | bytes 589832 | tf_op jit(solution)/shard_map/ppermute | solution.py:266
  83.7 5.9 %collective-permute-done.10.rest_2_ = bf16[2,384,128]{2,1,0:T(8,128)(2,1)S(1)} collective-permute-done((bf16[2,384,128]{2,1,0:T(8,128)(2,1)S(1)}, bf16[2,384,128]{2,1,0:T(8,128)(2,1)S(1)}, u32[]{:S(2)}, u32[]{:S(2)}) %collective-permute-start.10) | collective-permute-done | bytes 196640 | tf_op jit(solution)/shard_map/ppermute | solution.py:266
  89.6 3.4 %collective-permute-done.8.rest_0_ = bf16[2,384,128]{2,1,0:T(8,128)(2,1)S(1)} collective-permute-done((bf16[2,384,128]{2,1,0:T(8,128)(2,1)S(1)}, bf16[2,384,128]{2,1,0:T(8,128)(2,1)S(1)}, u32[]{:S(2)}, u32[]{:S(2)}) %collective-permute-start.8) | collective-permute-done | bytes 196640 | tf_op jit(solution)/shard_map/ppermute | solution.py:266
  93.0 2.1 %collective-permute-done.9.rest_1_ = bf16[2,384,128]{2,1,0:T(8,128)(2,1)S(1)} collective-permute-done((bf16[2,384,128]{2,1,0:T(8,128)(2,1)S(1)}, bf16[2,384,128]{2,1,0:T(8,128)(2,1)S(1)}, u32[]{:S(2)}, u32[]{:S(2)}) %collective-permute-start.9) | collective-permute-done | bytes 196640 | tf_op jit(solution)/shard_map/ppermute | solution.py:266
  98.9 9.1 %all-to-all-start.2 = ((bf16[32,128,128]{2,1,0:T(8,128)(2,1)}), bf16[32,128,128]{2,1,0:T(8,128)(2,1)S(1)}, u32[]{:S(2)}, u32[]{:S(2)}) async-start(bf16[32,128,128]{2,1,0:T(8,128)(2,1)} %get-tuple-element.46), calls=%async_computation.2 | async-start | bytes 2097152 | tf_op jit(solution)/shard_map/all_to_all | solution.py:312
  113.1 5.2 %attend_shared.1 = (bf16[2,128,128]{2,1,0:T(8,128)(2,1)}, bf16[2,128,128]{2,1,0:T(8,128)(2,1)}, bf16[2,128,128]{2,1,0:T(8,128)(2,1)}, bf16[2,128,128]{2,1,0:T(8,128)(2,1)}) custom-call(s32[4]{0:T(128)} %pad_add_fusion.pos_ref, s32[4,8,9]{2,1,0:T(8,128)} %fusion.10.lists_ref, bf16[8,400,128]{2,1,0:T(8,128)(2,1)} %copy-done, bf16[2,384,128]{2,1,0:T(8,128)(2,1)} %copy-done.7, ...), custom_call_target="tpu_custom_call" | custom-call | flops 536870912 | bytes 1572864 | tf_op jit(solution)/shard_map/attend_shared/pallas_call | solution.py:244
  118.3 2.7 %collective-permute-start.12 = (bf16[2,128,128]{2,1,0:T(8,128)(2,1)}, bf16[2,128,128]{2,1,0:T(8,128)(2,1)S(1)}, u32[]{:S(2)}, u32[]{:S(2)}) collective-permute-start(bf16[2,128,128]{2,1,0:T(8,128)(2,1)} %get-tuple-element.43), channel_id=1, source_target_pairs={{1,0},{2,1},{3,2},{0,3},{5,4},{6,5},{7,6},{4,7},{9,8},{10,9},{11,1... | collective-permute-start | bytes 196616 | tf_op jit(solution)/shard_map/ppermute | solution.py:266
  122.8 3.8 %collective-permute-done.12 = bf16[2,128,128]{2,1,0:T(8,128)(2,1)S(1)} collective-permute-done((bf16[2,128,128]{2,1,0:T(8,128)(2,1)}, bf16[2,128,128]{2,1,0:T(8,128)(2,1)S(1)}, u32[]{:S(2)}, u32[]{:S(2)}) %collective-permute-start.12) | collective-permute-done | bytes 65568 | tf_op jit(solution)/shard_map/ppermute | solution.py:266
  126.6 2.7 %collective-permute-done.13 = bf16[2,128,128]{2,1,0:T(8,128)(2,1)S(1)} collective-permute-done((bf16[2,128,128]{2,1,0:T(8,128)(2,1)}, bf16[2,128,128]{2,1,0:T(8,128)(2,1)S(1)}, u32[]{:S(2)}, u32[]{:S(2)}) %collective-permute-start.13) | collective-permute-done | bytes 65568 | tf_op jit(solution)/shard_map/ppermute | solution.py:266
  129.3 4.4 %collective-permute-done.14 = bf16[2,128,128]{2,1,0:T(8,128)(2,1)S(1)} collective-permute-done((bf16[2,128,128]{2,1,0:T(8,128)(2,1)}, bf16[2,128,128]{2,1,0:T(8,128)(2,1)S(1)}, u32[]{:S(2)}, u32[]{:S(2)}) %collective-permute-start.14) | collective-permute-done | bytes 65568 | tf_op jit(solution)/shard_map/ppermute | solution.py:266
  135.4 2.5 %all-to-all-done.2.q_ref = bf16[32,128,128]{2,1,0:T(8,128)(2,1)S(1)} async-done(((bf16[32,128,128]{2,1,0:T(8,128)(2,1)}), bf16[32,128,128]{2,1,0:T(8,128)(2,1)S(1)}, u32[]{:S(2)}, u32[]{:S(2)}) %all-to-all-start.2) | async-done | bytes 1048608 | tf_op jit(solution)/shard_map/all_to_all | solution.py:312
  139.0 6.5 %all-to-all-start.4 = ((bf16[8,128,128]{2,1,0:T(8,128)(2,1)}), bf16[8,128,128]{2,1,0:T(8,128)(2,1)S(1)}, u32[]{:S(2)}, u32[]{:S(2)}) async-start(bf16[8,128,128]{2,1,0:T(8,128)(2,1)} %bitcast.28), calls=%async_computation.4 | async-start | bytes 524288 | tf_op jit(solution)/shard_map/all_to_all | solution.py:321
  146.3 9.8 %attend_main.1 = bf16[32,128,128]{2,1,0:T(8,128)(2,1)} custom-call(s32[4]{0:T(128)} %pad_add_fusion.pos_ref, s32[4,8,9]{2,1,0:T(8,128)} %fusion.10.lists_ref, bf16[32,128,128]{2,1,0:T(8,128)(2,1)} %copy-done.5, bf16[32,256,128]{2,1,0:T(8,128)(2,1)} %bitcast.61, bf16[2,4,256,128]{3,2,1,0:T(8,128)(2,1)} %select_select_fusion.own_ref, ...), custom_call_target="tpu_custom_call" | custom-call | flops 2147483648 | bytes 3145728 | tf_op jit(solution)/shard_map/attend_main/pallas_call | solution.py:194
  156.2 39.0 %all_to_all.25.main_ref = bf16[32,128,128]{2,1,0:T(8,128)(2,1)S(1)} all-to-all(bf16[32,128,128]{2,1,0:T(8,128)(2,1)} %attend_main.1), channel_id=1, replica_groups=mesh['zl'=4,'x'=4,'c'=2,'zh'=2,'y'=4] {'zl','zh','y'}, dimensions={0} | all-to-all | bytes 2097152 | tf_op jit(solution)/shard_map/all_to_all | solution.py:326
  (77 shorter events, 26.2 us)
Async XLA Ops:
  4.2 29.3 %all-to-all-start = ((bf16[8,400,128]{2,1,0:T(8,128)(2,1)}), bf16[8,400,128]{2,1,0:T(8,128)(2,1)S(1)}, u32[]{:S(2)}, u32[]{:S(2)}) async-start(bf16[8,400,128]{2,1,0:T(8,128)(2,1)} %shared_rows.1), calls=%async_computation | async-start | bytes 1638400 | tf_op jit(solution)/shard_map/all_to_all | solution.py:296
  33.5 64.8 %copy-start = (bf16[8,400,128]{2,1,0:T(8,128)(2,1)}, bf16[8,400,128]{2,1,0:T(8,128)(2,1)S(1)}, u32[]{:S(2)}) copy-start(bf16[8,400,128]{2,1,0:T(8,128)(2,1)S(1)} %all-to-all-done.five_ref) | copy-start | bytes 2457604
  33.5 62.3 %all-to-all-start.1 = ((bf16[32,2,128,128]{3,2,1,0:T(8,128)(2,1)}), bf16[32,2,128,128]{3,2,1,0:T(8,128)(2,1)S(1)}, u32[]{:S(2)}, u32[]{:S(2)}) async-start(bf16[32,2,128,128]{3,2,1,0:T(8,128)(2,1)} %get-tuple-element.33), calls=%async_computation.1 | async-start | bytes 4194304 | tf_op jit(solution)/shard_map/all_to_all | solution.py:298
  45.9 1.4 collective-permute-start
  47.4 8.7 %collective-permute-start.1 = (bf16[2,256,128]{2,1,0:T(8,128)(2,1)S(1)}, bf16[2,256,128]{2,1,0:T(8,128)(2,1)S(1)}, u32[]{:S(2)}, u32[]{:S(2)}) collective-permute-start(bf16[2,256,128]{2,1,0:T(8,128)(2,1)S(1)} %fusion.9), channel_id=1, source_target_pairs={{16,0},{32,16},{48,32},{0,48},{17,1},{33,17},{49,33},{1,49},{18,2}... | collective-permute-start | bytes 393224 | tf_op jit(solution)/shard_map/ppermute | solution.py:266
  50.3 7.9 %collective-permute-start.2 = (bf16[2,256,128]{2,1,0:T(8,128)(2,1)S(1)}, bf16[2,256,128]{2,1,0:T(8,128)(2,1)S(1)}, u32[]{:S(2)}, u32[]{:S(2)}) collective-permute-start(bf16[2,256,128]{2,1,0:T(8,128)(2,1)S(1)} %fusion.9), channel_id=1, source_target_pairs={{32,0},{48,16},{0,32},{16,48},{33,1},{49,17},{1,33},{17,49},{34,2}... | collective-permute-start | bytes 393224 | tf_op jit(solution)/shard_map/ppermute | solution.py:266
  51.1 8.8 %collective-permute-start.3 = (bf16[2,256,128]{2,1,0:T(8,128)(2,1)S(1)}, bf16[2,256,128]{2,1,0:T(8,128)(2,1)S(1)}, u32[]{:S(2)}, u32[]{:S(2)}) collective-permute-start(bf16[2,256,128]{2,1,0:T(8,128)(2,1)S(1)} %fusion.9), channel_id=1, source_target_pairs={{48,0},{0,16},{16,32},{32,48},{49,1},{1,17},{17,33},{33,49},{50,2}... | collective-permute-start | bytes 393224 | tf_op jit(solution)/shard_map/ppermute | solution.py:266
  59.9 17.7 %collective-permute-start.4 = (bf16[2,256,128]{2,1,0:T(8,128)(2,1)S(1)}, bf16[2,256,128]{2,1,0:T(8,128)(2,1)S(1)}, u32[]{:S(2)}, u32[]{:S(2)}) collective-permute-start(bf16[2,256,128]{2,1,0:T(8,128)(2,1)S(1)} %select_select_fusion.1), channel_id=1, source_target_pairs={{1,0},{2,1},{3,2},{0,3},{5,4},{6,5},{7,6},{4,7},{9,8},{10,9},{11,1... | collective-permute-start | bytes 393224 | tf_op jit(solution)/shard_map/ppermute | solution.py:266
  62.7 14.9 %collective-permute-start.5 = (bf16[2,256,128]{2,1,0:T(8,128)(2,1)S(1)}, bf16[2,256,128]{2,1,0:T(8,128)(2,1)S(1)}, u32[]{:S(2)}, u32[]{:S(2)}) collective-permute-start(bf16[2,256,128]{2,1,0:T(8,128)(2,1)S(1)} %select_select_fusion.1), channel_id=1, source_target_pairs={{2,0},{3,1},{0,2},{1,3},{6,4},{7,5},{4,6},{5,7},{10,8},{11,9},{8,1... | collective-permute-start | bytes 393224 | tf_op jit(solution)/shard_map/ppermute | solution.py:266
  63.5 15.6 %collective-permute-start.6 = (bf16[2,256,128]{2,1,0:T(8,128)(2,1)S(1)}, bf16[2,256,128]{2,1,0:T(8,128)(2,1)S(1)}, u32[]{:S(2)}, u32[]{:S(2)}) collective-permute-start(bf16[2,256,128]{2,1,0:T(8,128)(2,1)S(1)} %select_select_fusion.1), channel_id=1, source_target_pairs={{3,0},{0,1},{1,2},{2,3},{7,4},{4,5},{5,6},{6,7},{11,8},{8,9},{9,10... | collective-permute-start | bytes 393224 | tf_op jit(solution)/shard_map/ppermute | solution.py:266
  79.3 16.6 %collective-permute-start.7 = (bf16[8,256,128]{2,1,0:T(8,128)(2,1)S(1)}, bf16[8,256,128]{2,1,0:T(8,128)(2,1)}, u32[]{:S(2)}, u32[]{:S(2)}) collective-permute-start(bf16[8,256,128]{2,1,0:T(8,128)(2,1)S(1)} %pad_maximum_fusion.rest_3_), channel_id=1, source_target_pairs={{8,0},{0,8},{9,1},{1,9},{10,2},{2,10},{11,3},{3,11},{12,4},{4,12},... | collective-permute-start | bytes 1572872 | tf_op jit(solution)/shard_map/ppermute | solution.py:266
  80.1 9.5 %collective-permute-start.10 = (bf16[2,384,128]{2,1,0:T(8,128)(2,1)S(1)}, bf16[2,384,128]{2,1,0:T(8,128)(2,1)S(1)}, u32[]{:S(2)}, u32[]{:S(2)}) collective-permute-start(bf16[2,384,128]{2,1,0:T(8,128)(2,1)S(1)} %get-tuple-element.59), channel_id=1, source_target_pairs={{3,0},{0,1},{1,2},{2,3},{7,4},{4,5},{5,6},{6,7},{11,8},{8,9},{9,10... | collective-permute-start | bytes 589832 | tf_op jit(solution)/shard_map/ppermute | solution.py:266
  80.1 12.9 %collective-permute-start.8 = (bf16[2,384,128]{2,1,0:T(8,128)(2,1)S(1)}, bf16[2,384,128]{2,1,0:T(8,128)(2,1)S(1)}, u32[]{:S(2)}, u32[]{:S(2)}) collective-permute-start(bf16[2,384,128]{2,1,0:T(8,128)(2,1)S(1)} %get-tuple-element.61), channel_id=1, source_target_pairs={{1,0},{2,1},{3,2},{0,3},{5,4},{6,5},{7,6},{4,7},{9,8},{10,9},{11,1... | collective-permute-start | bytes 589832 | tf_op jit(solution)/shard_map/ppermute | solution.py:266
  83.3 11.8 %collective-permute-start.9 = (bf16[2,384,128]{2,1,0:T(8,128)(2,1)S(1)}, bf16[2,384,128]{2,1,0:T(8,128)(2,1)S(1)}, u32[]{:S(2)}, u32[]{:S(2)}) collective-permute-start(bf16[2,384,128]{2,1,0:T(8,128)(2,1)S(1)} %get-tuple-element.60), channel_id=1, source_target_pairs={{2,0},{3,1},{0,2},{1,3},{6,4},{7,5},{4,6},{5,7},{10,8},{11,9},{8,1... | collective-permute-start | bytes 589832 | tf_op jit(solution)/shard_map/ppermute | solution.py:266
  97.7 10.3 %collective-permute-start.11 = (bf16[2,4,256,128]{3,2,1,0:T(8,128)(2,1)}, bf16[2,4,256,128]{3,2,1,0:T(8,128)(2,1)}, u32[]{:S(2)}, u32[]{:S(2)}) collective-permute-start(bf16[2,4,256,128]{3,2,1,0:T(8,128)(2,1)} %fusion.1), channel_id=1, source_target_pairs={{8,0},{0,8},{9,1},{1,9},{10,2},{2,10},{11,3},{3,11},{12,4},{4,12},... | collective-permute-start | bytes 1572872 | tf_op jit(solution)/shard_map/ppermute | solution.py:266
  98.9 38.9 %all-to-all-start.2 = ((bf16[32,128,128]{2,1,0:T(8,128)(2,1)}), bf16[32,128,128]{2,1,0:T(8,128)(2,1)S(1)}, u32[]{:S(2)}, u32[]{:S(2)}) async-start(bf16[32,128,128]{2,1,0:T(8,128)(2,1)} %get-tuple-element.46), calls=%async_computation.2 | async-start | bytes 2097152 | tf_op jit(solution)/shard_map/all_to_all | solution.py:312
  109.2 28.7 %collective-permute-start.15 = (bf16[2,4,256,128]{3,2,1,0:T(8,128)(2,1)S(1)}, bf16[2,4,256,128]{3,2,1,0:T(8,128)(2,1)S(1)}, u32[]{:S(2)}, u32[]{:S(2)}) collective-permute-start(bf16[2,4,256,128]{3,2,1,0:T(8,128)(2,1)S(1)} %fusion.4), channel_id=1, source_target_pairs={{16,0},{32,16},{48,32},{0,48},{17,1},{33,17},{49,33},{1,49},{18,2}... | collective-permute-start | bytes 1572872 | tf_op jit(solution)/shard_map/ppermute | solution.py:266
  111.1 26.8 %collective-permute-start.16 = (bf16[2,4,256,128]{3,2,1,0:T(8,128)(2,1)S(1)}, bf16[2,4,256,128]{3,2,1,0:T(8,128)(2,1)S(1)}, u32[]{:S(2)}, u32[]{:S(2)}) collective-permute-start(bf16[2,4,256,128]{3,2,1,0:T(8,128)(2,1)S(1)} %fusion.4), channel_id=1, source_target_pairs={{32,0},{48,16},{0,32},{16,48},{33,1},{49,17},{1,33},{17,49},{34,2}... | collective-permute-start | bytes 1572872 | tf_op jit(solution)/shard_map/ppermute | solution.py:266
  111.9 26.0 %collective-permute-start.17 = (bf16[2,4,256,128]{3,2,1,0:T(8,128)(2,1)S(1)}, bf16[2,4,256,128]{3,2,1,0:T(8,128)(2,1)S(1)}, u32[]{:S(2)}, u32[]{:S(2)}) collective-permute-start(bf16[2,4,256,128]{3,2,1,0:T(8,128)(2,1)S(1)} %fusion.4), channel_id=1, source_target_pairs={{48,0},{0,16},{16,32},{32,48},{49,1},{1,17},{17,33},{33,49},{50,2}... | collective-permute-start | bytes 1572872 | tf_op jit(solution)/shard_map/ppermute | solution.py:266
  118.3 8.2 %collective-permute-start.12 = (bf16[2,128,128]{2,1,0:T(8,128)(2,1)}, bf16[2,128,128]{2,1,0:T(8,128)(2,1)S(1)}, u32[]{:S(2)}, u32[]{:S(2)}) collective-permute-start(bf16[2,128,128]{2,1,0:T(8,128)(2,1)} %get-tuple-element.43), channel_id=1, source_target_pairs={{1,0},{2,1},{3,2},{0,3},{5,4},{6,5},{7,6},{4,7},{9,8},{10,9},{11,1... | collective-permute-start | bytes 196616 | tf_op jit(solution)/shard_map/ppermute | solution.py:266
  121.9 7.3 %collective-permute-start.13 = (bf16[2,128,128]{2,1,0:T(8,128)(2,1)}, bf16[2,128,128]{2,1,0:T(8,128)(2,1)S(1)}, u32[]{:S(2)}, u32[]{:S(2)}) collective-permute-start(bf16[2,128,128]{2,1,0:T(8,128)(2,1)} %get-tuple-element.44), channel_id=1, source_target_pairs={{2,0},{3,1},{0,2},{1,3},{6,4},{7,5},{4,6},{5,7},{10,8},{11,9},{8,1... | collective-permute-start | bytes 196616 | tf_op jit(solution)/shard_map/ppermute | solution.py:266
  126.6 7.1 %collective-permute-start.14 = (bf16[2,128,128]{2,1,0:T(8,128)(2,1)}, bf16[2,128,128]{2,1,0:T(8,128)(2,1)S(1)}, u32[]{:S(2)}, u32[]{:S(2)}) collective-permute-start(bf16[2,128,128]{2,1,0:T(8,128)(2,1)} %get-tuple-element.45), channel_id=1, source_target_pairs={{3,0},{0,1},{1,2},{2,3},{7,4},{4,5},{5,6},{6,7},{11,8},{8,9},{9,10... | collective-permute-start | bytes 196616 | tf_op jit(solution)/shard_map/ppermute | solution.py:266
  139.0 6.5 %collective-permute-start.18 = (bf16[2,4,256,128]{3,2,1,0:T(8,128)(2,1)}, bf16[2,4,256,128]{3,2,1,0:T(8,128)(2,1)S(1)}, u32[]{:S(2)}, u32[]{:S(2)}) collective-permute-start(bf16[2,4,256,128]{3,2,1,0:T(8,128)(2,1)} %select_select_fusion.own_ref), channel_id=1, source_target_pairs={{8,0},{0,8},{9,1},{1,9},{10,2},{2,10},{11,3},{3,11},{12,4},{4,12},... | collective-permute-start | bytes 1572872 | tf_op jit(solution)/shard_map/ppermute | solution.py:266
  139.0 17.2 %all-to-all-start.4 = ((bf16[8,128,128]{2,1,0:T(8,128)(2,1)}), bf16[8,128,128]{2,1,0:T(8,128)(2,1)S(1)}, u32[]{:S(2)}, u32[]{:S(2)}) async-start(bf16[8,128,128]{2,1,0:T(8,128)(2,1)} %bitcast.28), calls=%async_computation.4 | async-start | bytes 524288 | tf_op jit(solution)/shard_map/all_to_all | solution.py:321
  (10 other events, 32.0 us)

commit v3 on v2

--- a/solution.py
+++ b/solution.py
@@ -198,7 +198,7 @@
         out_specs=blocks,
         out_shape=jax.ShapeDtypeStruct(q_all.shape, BF16),
         scratch_shapes=[pltpu.VMEM((SLOTS, 2 * BLOCK, HD), BF16), pltpu.SemaphoreType.DMA((5,))],
-        compiler_params=pltpu.CompilerParams(vmem_limit_bytes=VMEM),
+        compiler_params=pltpu.CompilerParams(vmem_limit_bytes=HALF),
         cost_estimate=pl.CostEstimate(
             flops=32 * 4 * BLOCK * LISTED * BLOCK * HD,
             bytes_accessed=4 * SLOTS * BLOCK * HD,
@@ -252,7 +252,7 @@
             pltpu.VMEM((24, 2 * BLOCK, HD), BF16),
             pltpu.SemaphoreType.DMA((10,)),
         ],
-        compiler_params=pltpu.CompilerParams(vmem_limit_bytes=VMEM),
+        compiler_params=pltpu.CompilerParams(vmem_limit_bytes=HALF),
         cost_estimate=pl.CostEstimate(
             flops=8 * 4 * BLOCK * LISTED * BLOCK * HD,
             bytes_accessed=4 * 24 * BLOCK * HD,
@@ -264,6 +264,26 @@
 
 def shifted(x, axis, size, by):
     return lax.ppermute(x, axis, [((i + by) % size, i) for i in range(size)])
+
+
+def ring_kernel(me_ref, *rest):
+    parts, out_ref = rest[:-1], rest[-1]
+    for r, part in enumerate(parts):
+        out_ref[lax.rem(me_ref[0] - r + len(parts), len(parts))] = part[...]
+
+
+def ordered(me, parts, name):
+    count, shape = len(parts), parts[0].shape
+    zeros = (0,) * len(shape)
+    return pl.pallas_call(
+        ring_kernel,
+        grid=(1,),
+        in_specs=[SMEM] + [pl.BlockSpec(shape, lambda i: zeros)] * count,
+        out_specs=pl.BlockSpec((count, *shape), lambda i: (0, *zeros)),
+        out_shape=jax.ShapeDtypeStruct((count, *shape), BF16),
+        compiler_params=pltpu.CompilerParams(vmem_limit_bytes=HALF),
+        name=name,
+    )(me.reshape(1), *parts)
 
 
 def core_half(by_zl, at_zl, at_c):
@@ -306,6 +326,7 @@
     for by in (1, 2, 3):
         view = lax.dynamic_index_in_dim(by_view[:, :, : 3 * BLOCK], (y - by) % 4, 0, keepdims=False)
         got.append(shifted(view, "y", 4, by))
+    half, *got = lax.optimization_barrier((half, *got))
     near = jnp.concatenate([half] + [shifted(half, "y", 4, by) for by in (1, 2, 3)], axis=0)
     far = shifted(near, "c", 2, 1)
     kv_all, q_rows, near, far, *got = lax.optimization_barrier((kv_all, q_rows, near, far, *got))
@@ -315,8 +336,8 @@
     half, near = lax.optimization_barrier((half, near))
     others = along_x(half)
     parts = attend_shared(pos, lists, five, got, near, far)
-    back = jnp.stack([parts[0]] + [shifted(parts[d], "y", 4, -d) for d in (3, 2, 1)])
-    shared = lax.dynamic_slice_in_dim(jnp.concatenate([back, back]), 4 - y, 4, 0).reshape(PLANES, BLOCK, HD)
+    shared = [parts[0]] + [shifted(parts[d], "y", 4, -d) for d in (1, 2, 3)]
+    shared = ordered(y, shared, "order_views").reshape(PLANES, BLOCK, HD)
     shared, q_all = lax.optimization_barrier((shared, q_all))
     home = lax.all_to_all(shared, PLANE, 0, 0, tiled=True)
     shared, q_all, *others = lax.optimization_barrier((shared, q_all, *others))

time: 198 us -> 194 us (0.980)
  starting transfers between devices: 52.3 us -> 57 us
  Pallas kernels: 25.9 us -> 22.7 us
  blocking collectives: 39 us -> 36.8 us
    ppermute x19, waiting for transfers between devices: 46.4 us -> 42.4 us  [shifted(): return lax.ppermute(x, axis, [((i + by) % size, i) for i in range(size)])]
    ppermute x19, starting transfers between devices: 20.4 us -> 23.5 us  [shifted(): return lax.ppermute(x, axis, [((i + by) % size, i) for i in range(size)])]
    pallas_call x1, Pallas kernels: 9.83 us -> 7.4 us  [attend_main(): pl.pallas_call(main_kernel, grid=(4,), in_specs=[SMEM, SMEM, blocks, ANY,...]
    all_to_all x1, blocking collectives: 39 us -> 36.8 us  [shards(): main = lax.all_to_all(mixed, EVERY, 0, 0, tiled=True)]
    all_to_all x1, waiting for transfers between devices: 0.09 us -> 2.33 us  [shards(): home = lax.all_to_all(shared, PLANE, 0, 0, tiled=True)]
    unnamed x29 -> x23, local copies, waits for them, and re-layouts: 4.66 us -> 5.64 us
  transfers between devices with their start and end apart: 23 -> 23, of which waited for: 15 -> 19; matrix products, arithmetic and copies ran while one was open for 3% -> 1% of each run, Pallas kernels for 10% -> 9%
where the time goes in v3:
time: 194 us; the launch traced here: 193 us
  waiting for transfers between devices  63.7 us (33%)
  starting transfers between devices  57 us (29%)
  blocking collectives  36.8 us (19%)
  Pallas kernels  22.7 us (12%)
  local copies, waits for them, and re-layouts  6.47 us (3%)
  between operations  3.56 us (2%)
  other arithmetic  2.99 us (2%)
    ppermute x19, waiting for transfers between devices, shifted(): return lax.ppermute(x, axis, [((i + by) % size, i) for i in range(size)])  42.4 us
    all_to_all x1, blocking collectives, shards(): main = lax.all_to_all(mixed, EVERY, 0, 0, tiled=True)  36.8 us
    ppermute x19, starting transfers between devices, shifted(): return lax.ppermute(x, axis, [((i + by) % size, i) for i in range(size)])  23.5 us
    all_to_all x1, waiting for transfers between devices, shards(): five = lax.all_to_all(five, PLANE, 0, 0, tiled=True)  15.9 us
    all_to_all x1, starting transfers between devices, shards(): q_all = lax.all_to_all(q_rows, EVERY, 0, 0, tiled=True)  9.89 us
    all_to_all x1, starting transfers between devices, shards(): five = lax.all_to_all(five, PLANE, 0, 0, tiled=True)  8.57 us
    all_to_all x1, starting transfers between devices, shards(): lax.all_to_all(kv_rows, EVERY, 0, 0, tiled=True).reshape(32, 2 * BLOCK, HD)  7.87 us
    pallas_call x1, Pallas kernels, attend_main(): pl.pallas_call(main_kernel, grid=(4,), in_specs=[SMEM, SMEM, blocks, ANY,...  7.4 us
  transfers between devices with their start and end apart: 23, of which 19 were waited for; matrix products, arithmetic and copies ran while one was open for 1% of the time, Pallas kernels for 9%

profile of v3, /device:TPU:32, one launch (start us, length us, event | category | flops | bytes accessed | tf_op | source)
XLA Modules:
  0.0 193.2 jit_solution(6992738234345612457)
XLA Ops:
  0.0 4.2 %shared_rows.1 = bf16[8,400,128]{2,1,0:T(8,128)(2,1)} custom-call(bf16[128,5120]{1,0:T(8,128)(2,1)} %q_ref.3, bf16[128,5120]{1,0:T(8,128)(2,1)} %k_ref.3, bf16[128,5120]{1,0:T(8,128)(2,1)} %v_ref.3, f32[1,5120]{1,0:T(1,128)} %bitcast.50, f32[1,5120]{1,0:T(1,128)} %bitcast.52, s32[1,8,8]{2,1,0:T(8,128)} %ids_ref.1, s32[1,8]{1,0:T(1,128)} %cnt_ref.1), custom_call_target="tpu_custom_call" | custom-call | tf_op jit(solution)/shard_map/shared_rows/pallas_call | solution.py:85
  4.2 8.6 %all-to-all-start = ((bf16[8,400,128]{2,1,0:T(8,128)(2,1)}), bf16[8,400,128]{2,1,0:T(8,128)(2,1)S(1)}, u32[]{:S(2)}, u32[]{:S(2)}) async-start(bf16[8,400,128]{2,1,0:T(8,128)(2,1)} %shared_rows.1), calls=%async_computation | async-start | bytes 1638400 | tf_op jit(solution)/shard_map/all_to_all | solution.py:316
  12.8 4.9 %own_rows.1 = (bf16[32,128,128]{2,1,0:T(8,128)(2,1)}, bf16[32,2,128,128]{3,2,1,0:T(8,128)(2,1)}) custom-call(bf16[128,5120]{1,0:T(8,128)(2,1)} %q_ref.3, bf16[128,5120]{1,0:T(8,128)(2,1)} %k_ref.3, bf16[128,5120]{1,0:T(8,128)(2,1)} %v_ref.3, f32[1,5120]{1,0:T(1,128)} %bitcast.51, f32[1,5120]{1,0:T(1,128)} %bitcast.53), custom_call_target="tpu_custom_call" | custom-call | tf_op jit(solution)/shard_map/own_rows/pallas_call | solution.py:94
  17.7 15.9 %all-to-all-done.five_ref = bf16[8,400,128]{2,1,0:T(8,128)(2,1)S(1)} async-done(((bf16[8,400,128]{2,1,0:T(8,128)(2,1)}), bf16[8,400,128]{2,1,0:T(8,128)(2,1)S(1)}, u32[]{:S(2)}, u32[]{:S(2)}) %all-to-all-start) | async-done | bytes 819232 | tf_op jit(solution)/shard_map/all_to_all | solution.py:316
  33.5 7.9 %all-to-all-start.1 = ((bf16[32,2,128,128]{3,2,1,0:T(8,128)(2,1)}), bf16[32,2,128,128]{3,2,1,0:T(8,128)(2,1)S(1)}, u32[]{:S(2)}, u32[]{:S(2)}) async-start(bf16[32,2,128,128]{3,2,1,0:T(8,128)(2,1)} %get-tuple-element.37), calls=%async_computation.1 | async-start | bytes 4194304 | tf_op jit(solution)/shard_map/all_to_all | solution.py:318
  47.0 2.8 %collective-permute-start.1 = (bf16[2,256,128]{2,1,0:T(8,128)(2,1)S(1)}, bf16[2,256,128]{2,1,0:T(8,128)(2,1)S(1)}, u32[]{:S(2)}, u32[]{:S(2)}) collective-permute-start(bf16[2,256,128]{2,1,0:T(8,128)(2,1)S(1)} %fusion.9), channel_id=1, source_target_pairs={{16,0},{32,16},{48,32},{0,48},{17,1},{33,17},{49,33},{1,49},{18,2}... | collective-permute-start | bytes 393224 | tf_op jit(solution)/shard_map/ppermute | solution.py:266
  51.6 2.8 %collective-permute-start.4 = (bf16[2,384,128]{2,1,0:T(8,128)(2,1)S(1)}, bf16[2,384,128]{2,1,0:T(8,128)(2,1)S(1)}, u32[]{:S(2)}, u32[]{:S(2)}) collective-permute-start(bf16[2,384,128]{2,1,0:T(8,128)(2,1)S(1)} %get-tuple-element.69), channel_id=1, source_target_pairs={{1,0},{2,1},{3,2},{0,3},{5,4},{6,5},{7,6},{4,7},{9,8},{10,9},{11,1... | collective-permute-start | bytes 589832 | tf_op jit(solution)/shard_map/ppermute | solution.py:266
  59.5 12.4 %collective-permute-done.4.rest_0_ = bf16[2,384,128]{2,1,0:T(8,128)(2,1)S(1)} collective-permute-done((bf16[2,384,128]{2,1,0:T(8,128)(2,1)S(1)}, bf16[2,384,128]{2,1,0:T(8,128)(2,1)S(1)}, u32[]{:S(2)}, u32[]{:S(2)}) %collective-permute-start.4) | collective-permute-done | bytes 196640 | tf_op jit(solution)/shard_map/ppermute | solution.py:266
  71.9 4.7 %collective-permute-done.6.rest_2_ = bf16[2,384,128]{2,1,0:T(8,128)(2,1)S(1)} collective-permute-done((bf16[2,384,128]{2,1,0:T(8,128)(2,1)S(1)}, bf16[2,384,128]{2,1,0:T(8,128)(2,1)S(1)}, u32[]{:S(2)}, u32[]{:S(2)}) %collective-permute-start.6) | collective-permute-done | bytes 196640 | tf_op jit(solution)/shard_map/ppermute | solution.py:266
  76.7 2.9 %collective-permute-start.7 = (bf16[2,256,128]{2,1,0:T(8,128)(2,1)S(1)}, bf16[2,256,128]{2,1,0:T(8,128)(2,1)S(1)}, u32[]{:S(2)}, u32[]{:S(2)}) collective-permute-start(bf16[2,256,128]{2,1,0:T(8,128)(2,1)S(1)} %select_select_fusion.1), channel_id=1, source_target_pairs={{1,0},{2,1},{3,2},{0,3},{5,4},{6,5},{7,6},{4,7},{9,8},{10,9},{11,1... | collective-permute-start | bytes 393224 | tf_op jit(solution)/shard_map/ppermute | solution.py:266
  80.6 5.5 %collective-permute-done.7 = bf16[2,256,128]{2,1,0:T(8,128)(2,1)S(1)} collective-permute-done((bf16[2,256,128]{2,1,0:T(8,128)(2,1)S(1)}, bf16[2,256,128]{2,1,0:T(8,128)(2,1)S(1)}, u32[]{:S(2)}, u32[]{:S(2)}) %collective-permute-start.7) | collective-permute-done | bytes 131104 | tf_op jit(solution)/shard_map/ppermute | solution.py:266
  92.9 9.9 %all-to-all-start.2 = ((bf16[32,128,128]{2,1,0:T(8,128)(2,1)}), bf16[32,128,128]{2,1,0:T(8,128)(2,1)}, u32[]{:S(2)}, u32[]{:S(2)}) async-start(bf16[32,128,128]{2,1,0:T(8,128)(2,1)} %get-tuple-element.54), calls=%async_computation.2 | async-start | bytes 2097152 | tf_op jit(solution)/shard_map/all_to_all | solution.py:333
  103.0 1.9 collective-permute-done.11
  105.9 2.4 %collective-permute-start.15 = (bf16[2,4,256,128]{3,2,1,0:T(8,128)(2,1)}, bf16[2,4,256,128]{3,2,1,0:T(8,128)(2,1)}, u32[]{:S(2)}, u32[]{:S(2)}) collective-permute-start(bf16[2,4,256,128]{3,2,1,0:T(8,128)(2,1)} %fusion.4), channel_id=1, source_target_pairs={{16,0},{32,16},{48,32},{0,48},{17,1},{33,17},{49,33},{1,49},{18,2}... | collective-permute-start | bytes 1572872 | tf_op jit(solution)/shard_map/ppermute | solution.py:266
  114.4 3.7 %attend_shared.1 = (bf16[2,128,128]{2,1,0:T(8,128)(2,1)S(1)}, bf16[2,128,128]{2,1,0:T(8,128)(2,1)S(1)}, bf16[2,128,128]{2,1,0:T(8,128)(2,1)S(1)}, bf16[2,128,128]{2,1,0:T(8,128)(2,1)S(1)}) custom-call(s32[4]{0:T(128)S(1)} %pad_add_fusion.pos_ref, s32[4,8,9]{2,1,0:T(8,128)S(1)} %fusion.10.lists_ref, bf16[8,400,128]{2,1,0:T(8,128)(2,1)S(1)} %all-to-all-done.five_ref, ...), custom_call_target="tpu_custom_call" | custom-call | flops 536870912 | bytes 1572864 | tf_op jit(solution)/shard_map/attend_shared/pallas_call | solution.py:244
  119.6 2.7 %collective-permute-start.13 = (bf16[2,128,128]{2,1,0:T(8,128)(2,1)S(1)}, bf16[2,128,128]{2,1,0:T(8,128)(2,1)S(1)}, u32[]{:S(2)}, u32[]{:S(2)}) collective-permute-start(bf16[2,128,128]{2,1,0:T(8,128)(2,1)S(1)} %get-tuple-element.52), channel_id=1, source_target_pairs={{2,0},{3,1},{0,2},{1,3},{6,4},{7,5},{4,6},{5,7},{10,8},{11,9},{8,1... | collective-permute-start | bytes 196616 | tf_op jit(solution)/shard_map/ppermute | solution.py:266
  122.3 2.5 %collective-permute-done.12.rest_1_ = bf16[2,128,128]{2,1,0:T(8,128)(2,1)S(1)} collective-permute-done((bf16[2,128,128]{2,1,0:T(8,128)(2,1)S(1)}, bf16[2,128,128]{2,1,0:T(8,128)(2,1)S(1)}, u32[]{:S(2)}, u32[]{:S(2)}) %collective-permute-start.12) | collective-permute-done | bytes 65568 | tf_op jit(solution)/shard_map/ppermute | solution.py:266
  125.9 3.2 %collective-permute-done.14.rest_3_ = bf16[2,128,128]{2,1,0:T(8,128)(2,1)S(1)} collective-permute-done((bf16[2,128,128]{2,1,0:T(8,128)(2,1)S(1)}, bf16[2,128,128]{2,1,0:T(8,128)(2,1)S(1)}, u32[]{:S(2)}, u32[]{:S(2)}) %collective-permute-start.14) | collective-permute-done | bytes 65568 | tf_op jit(solution)/shard_map/ppermute | solution.py:266
  129.8 2.6 %all-to-all-done.2.q_ref = bf16[32,128,128]{2,1,0:T(8,128)(2,1)} async-done(((bf16[32,128,128]{2,1,0:T(8,128)(2,1)}), bf16[32,128,128]{2,1,0:T(8,128)(2,1)}, u32[]{:S(2)}, u32[]{:S(2)}) %all-to-all-start.2) | async-done | bytes 1048608 | tf_op jit(solution)/shard_map/all_to_all | solution.py:333
  132.4 2.6 %collective-permute-done.17 = bf16[2,4,256,128]{3,2,1,0:T(8,128)(2,1)} collective-permute-done((bf16[2,4,256,128]{3,2,1,0:T(8,128)(2,1)}, bf16[2,4,256,128]{3,2,1,0:T(8,128)(2,1)}, u32[]{:S(2)}, u32[]{:S(2)}) %collective-permute-start.17) | collective-permute-done | bytes 524320 | tf_op jit(solution)/shard_map/ppermute | solution.py:266
  136.8 7.2 %all-to-all-start.4 = ((bf16[8,128,128]{2,1,0:T(8,128)(2,1)}), bf16[8,128,128]{2,1,0:T(8,128)(2,1)S(1)}, u32[]{:S(2)}, u32[]{:S(2)}) async-start(bf16[8,128,128]{2,1,0:T(8,128)(2,1)} %bitcast.24), calls=%async_computation.4 | async-start | bytes 524288 | tf_op jit(solution)/shard_map/all_to_all | solution.py:342
  144.0 7.4 %attend_main.1 = bf16[32,128,128]{2,1,0:T(8,128)(2,1)S(1)} custom-call(s32[4]{0:T(128)S(1)} %pad_add_fusion.pos_ref, s32[4,8,9]{2,1,0:T(8,128)S(1)} %fusion.10.lists_ref, bf16[32,128,128]{2,1,0:T(8,128)(2,1)} %all-to-all-done.2.q_ref, bf16[32,256,128]{2,1,0:T(8,128)(2,1)S(1)} %bitcast.49, bf16[2,4,256,128]{3,2,1,0:T(8,128)(2,1)S(1)} %select_select_fusion.own_ref, ...), custom_call_target="tpu_custom_call" | custom-call | flops 2147483648 | bytes 3145728 | tf_op jit(solution)/shard_map/attend_main/pallas_call | solution.py:194
  152.4 2.3 %all-to-all-done.4.five_ref = bf16[8,128,128]{2,1,0:T(8,128)(2,1)S(1)} async-done(((bf16[8,128,128]{2,1,0:T(8,128)(2,1)}), bf16[8,128,128]{2,1,0:T(8,128)(2,1)S(1)}, u32[]{:S(2)}, u32[]{:S(2)}) %all-to-all-start.4) | async-done | bytes 262176 | tf_op jit(solution)/shard_map/all_to_all | solution.py:342
  154.7 36.8 %all_to_all.25.main_ref = bf16[32,128,128]{2,1,0:T(8,128)(2,1)S(1)} all-to-all(bf16[32,128,128]{2,1,0:T(8,128)(2,1)} %copy-done), channel_id=1, replica_groups=mesh['zl'=4,'x'=4,'c'=2,'zh'=2,'y'=4] {'zl','zh','y'}, dimensions={0} | all-to-all | bytes 2097152 | tf_op jit(solution)/shard_map/all_to_all | solution.py:347
  (70 shorter events, 32.0 us)
Async XLA Ops:
  4.2 29.3 %all-to-all-start = ((bf16[8,400,128]{2,1,0:T(8,128)(2,1)}), bf16[8,400,128]{2,1,0:T(8,128)(2,1)S(1)}, u32[]{:S(2)}, u32[]{:S(2)}) async-start(bf16[8,400,128]{2,1,0:T(8,128)(2,1)} %shared_rows.1), calls=%async_computation | async-start | bytes 1638400 | tf_op jit(solution)/shard_map/all_to_all | solution.py:316
  33.5 59.4 %all-to-all-start.1 = ((bf16[32,2,128,128]{3,2,1,0:T(8,128)(2,1)}), bf16[32,2,128,128]{3,2,1,0:T(8,128)(2,1)S(1)}, u32[]{:S(2)}, u32[]{:S(2)}) async-start(bf16[32,2,128,128]{3,2,1,0:T(8,128)(2,1)} %get-tuple-element.37), calls=%async_computation.1 | async-start | bytes 4194304 | tf_op jit(solution)/shard_map/all_to_all | solution.py:318
  45.5 1.4 collective-permute-start
  47.0 8.7 %collective-permute-start.1 = (bf16[2,256,128]{2,1,0:T(8,128)(2,1)S(1)}, bf16[2,256,128]{2,1,0:T(8,128)(2,1)S(1)}, u32[]{:S(2)}, u32[]{:S(2)}) collective-permute-start(bf16[2,256,128]{2,1,0:T(8,128)(2,1)S(1)} %fusion.9), channel_id=1, source_target_pairs={{16,0},{32,16},{48,32},{0,48},{17,1},{33,17},{49,33},{1,49},{18,2}... | collective-permute-start | bytes 393224 | tf_op jit(solution)/shard_map/ppermute | solution.py:266
  49.8 7.9 %collective-permute-start.2 = (bf16[2,256,128]{2,1,0:T(8,128)(2,1)S(1)}, bf16[2,256,128]{2,1,0:T(8,128)(2,1)S(1)}, u32[]{:S(2)}, u32[]{:S(2)}) collective-permute-start(bf16[2,256,128]{2,1,0:T(8,128)(2,1)S(1)} %fusion.9), channel_id=1, source_target_pairs={{32,0},{48,16},{0,32},{16,48},{33,1},{49,17},{1,33},{17,49},{34,2}... | collective-permute-start | bytes 393224 | tf_op jit(solution)/shard_map/ppermute | solution.py:266
  50.6 8.8 %collective-permute-start.3 = (bf16[2,256,128]{2,1,0:T(8,128)(2,1)S(1)}, bf16[2,256,128]{2,1,0:T(8,128)(2,1)S(1)}, u32[]{:S(2)}, u32[]{:S(2)}) collective-permute-start(bf16[2,256,128]{2,1,0:T(8,128)(2,1)S(1)} %fusion.9), channel_id=1, source_target_pairs={{48,0},{0,16},{16,32},{32,48},{49,1},{1,17},{17,33},{33,49},{50,2}... | collective-permute-start | bytes 393224 | tf_op jit(solution)/shard_map/ppermute | solution.py:266
  51.6 20.3 %collective-permute-start.4 = (bf16[2,384,128]{2,1,0:T(8,128)(2,1)S(1)}, bf16[2,384,128]{2,1,0:T(8,128)(2,1)S(1)}, u32[]{:S(2)}, u32[]{:S(2)}) collective-permute-start(bf16[2,384,128]{2,1,0:T(8,128)(2,1)S(1)} %get-tuple-element.69), channel_id=1, source_target_pairs={{1,0},{2,1},{3,2},{0,3},{5,4},{6,5},{7,6},{4,7},{9,8},{10,9},{11,1... | collective-permute-start | bytes 589832 | tf_op jit(solution)/shard_map/ppermute | solution.py:266
  54.4 17.5 %collective-permute-start.5 = (bf16[2,384,128]{2,1,0:T(8,128)(2,1)S(1)}, bf16[2,384,128]{2,1,0:T(8,128)(2,1)S(1)}, u32[]{:S(2)}, u32[]{:S(2)}) collective-permute-start(bf16[2,384,128]{2,1,0:T(8,128)(2,1)S(1)} %get-tuple-element.68), channel_id=1, source_target_pairs={{2,0},{3,1},{0,2},{1,3},{6,4},{7,5},{4,6},{5,7},{10,8},{11,9},{8,1... | collective-permute-start | bytes 589832 | tf_op jit(solution)/shard_map/ppermute | solution.py:266
  55.7 20.9 %collective-permute-start.6 = (bf16[2,384,128]{2,1,0:T(8,128)(2,1)S(1)}, bf16[2,384,128]{2,1,0:T(8,128)(2,1)S(1)}, u32[]{:S(2)}, u32[]{:S(2)}) collective-permute-start(bf16[2,384,128]{2,1,0:T(8,128)(2,1)S(1)} %get-tuple-element.67), channel_id=1, source_target_pairs={{3,0},{0,1},{1,2},{2,3},{7,4},{4,5},{5,6},{6,7},{11,8},{8,9},{9,10... | collective-permute-start | bytes 589832 | tf_op jit(solution)/shard_map/ppermute | solution.py:266
  71.9 17.7 %copy-start.5 = (bf16[2,384,128]{2,1,0:T(8,128)(2,1)}, bf16[2,384,128]{2,1,0:T(8,128)(2,1)S(1)}, u32[]{:S(2)}) copy-start(bf16[2,384,128]{2,1,0:T(8,128)(2,1)S(1)} %collective-permute-done.5.rest_1_) | copy-start | bytes 589828
  76.7 9.5 %collective-permute-start.7 = (bf16[2,256,128]{2,1,0:T(8,128)(2,1)S(1)}, bf16[2,256,128]{2,1,0:T(8,128)(2,1)S(1)}, u32[]{:S(2)}, u32[]{:S(2)}) collective-permute-start(bf16[2,256,128]{2,1,0:T(8,128)(2,1)S(1)} %select_select_fusion.1), channel_id=1, source_target_pairs={{1,0},{2,1},{3,2},{0,3},{5,4},{6,5},{7,6},{4,7},{9,8},{10,9},{11,1... | collective-permute-start | bytes 393224 | tf_op jit(solution)/shard_map/ppermute | solution.py:266
  79.6 8.3 %collective-permute-start.8 = (bf16[2,256,128]{2,1,0:T(8,128)(2,1)S(1)}, bf16[2,256,128]{2,1,0:T(8,128)(2,1)S(1)}, u32[]{:S(2)}, u32[]{:S(2)}) collective-permute-start(bf16[2,256,128]{2,1,0:T(8,128)(2,1)S(1)} %select_select_fusion.1), channel_id=1, source_target_pairs={{2,0},{3,1},{0,2},{1,3},{6,4},{7,5},{4,6},{5,7},{10,8},{11,9},{8,1... | collective-permute-start | bytes 393224 | tf_op jit(solution)/shard_map/ppermute | solution.py:266
  79.6 9.9 %collective-permute-start.9 = (bf16[2,256,128]{2,1,0:T(8,128)(2,1)S(1)}, bf16[2,256,128]{2,1,0:T(8,128)(2,1)S(1)}, u32[]{:S(2)}, u32[]{:S(2)}) collective-permute-start(bf16[2,256,128]{2,1,0:T(8,128)(2,1)S(1)} %select_select_fusion.1), channel_id=1, source_target_pairs={{3,0},{0,1},{1,2},{2,3},{7,4},{4,5},{5,6},{6,7},{11,8},{8,9},{9,10... | collective-permute-start | bytes 393224 | tf_op jit(solution)/shard_map/ppermute | solution.py:266
  89.6 2.0 %collective-permute-start.10 = (bf16[8,256,128]{2,1,0:T(8,128)(2,1)S(1)}, bf16[8,256,128]{2,1,0:T(8,128)(2,1)S(1)}, u32[]{:S(2)}, u32[]{:S(2)}) collective-permute-start(bf16[8,256,128]{2,1,0:T(8,128)(2,1)S(1)} %constant_dynamic-update-slice_fusion.rest_3_), channel_id=1, source_target_pairs={{8,0},{0,8},{9,1},{1,9},{10,2},{2,10},{11,3},{3,11},{12,4},{4,12},... | collective-permute-start | bytes 1572872 | tf_op jit(solution)/shard_map/ppermute | solution.py:266
  92.9 39.5 %all-to-all-start.2 = ((bf16[32,128,128]{2,1,0:T(8,128)(2,1)}), bf16[32,128,128]{2,1,0:T(8,128)(2,1)}, u32[]{:S(2)}, u32[]{:S(2)}) async-start(bf16[32,128,128]{2,1,0:T(8,128)(2,1)} %get-tuple-element.54), calls=%async_computation.2 | async-start | bytes 2097152 | tf_op jit(solution)/shard_map/all_to_all | solution.py:333
  102.9 2.0 %collective-permute-start.11 = (bf16[2,4,256,128]{3,2,1,0:T(8,128)(2,1)S(1)}, bf16[2,4,256,128]{3,2,1,0:T(8,128)(2,1)S(1)}, u32[]{:S(2)}, u32[]{:S(2)}) collective-permute-start(bf16[2,4,256,128]{3,2,1,0:T(8,128)(2,1)S(1)} %fusion.1), channel_id=1, source_target_pairs={{8,0},{0,8},{9,1},{1,9},{10,2},{2,10},{11,3},{3,11},{12,4},{4,12},... | collective-permute-start | bytes 1572872 | tf_op jit(solution)/shard_map/ppermute | solution.py:266
  105.9 26.5 %collective-permute-start.15 = (bf16[2,4,256,128]{3,2,1,0:T(8,128)(2,1)}, bf16[2,4,256,128]{3,2,1,0:T(8,128)(2,1)}, u32[]{:S(2)}, u32[]{:S(2)}) collective-permute-start(bf16[2,4,256,128]{3,2,1,0:T(8,128)(2,1)} %fusion.4), channel_id=1, source_target_pairs={{16,0},{32,16},{48,32},{0,48},{17,1},{33,17},{49,33},{1,49},{18,2}... | collective-permute-start | bytes 1572872 | tf_op jit(solution)/shard_map/ppermute | solution.py:266
  108.2 24.1 %collective-permute-start.16 = (bf16[2,4,256,128]{3,2,1,0:T(8,128)(2,1)}, bf16[2,4,256,128]{3,2,1,0:T(8,128)(2,1)}, u32[]{:S(2)}, u32[]{:S(2)}) collective-permute-start(bf16[2,4,256,128]{3,2,1,0:T(8,128)(2,1)} %fusion.4), channel_id=1, source_target_pairs={{32,0},{48,16},{0,32},{16,48},{33,1},{49,17},{1,33},{17,49},{34,2}... | collective-permute-start | bytes 1572872 | tf_op jit(solution)/shard_map/ppermute | solution.py:266
  109.7 25.2 %collective-permute-start.17 = (bf16[2,4,256,128]{3,2,1,0:T(8,128)(2,1)}, bf16[2,4,256,128]{3,2,1,0:T(8,128)(2,1)}, u32[]{:S(2)}, u32[]{:S(2)}) collective-permute-start(bf16[2,4,256,128]{3,2,1,0:T(8,128)(2,1)} %fusion.4), channel_id=1, source_target_pairs={{48,0},{0,16},{16,32},{32,48},{49,1},{1,17},{17,33},{33,49},{50,2}... | collective-permute-start | bytes 1572872 | tf_op jit(solution)/shard_map/ppermute | solution.py:266
  118.0 6.8 %collective-permute-start.12 = (bf16[2,128,128]{2,1,0:T(8,128)(2,1)S(1)}, bf16[2,128,128]{2,1,0:T(8,128)(2,1)S(1)}, u32[]{:S(2)}, u32[]{:S(2)}) collective-permute-start(bf16[2,128,128]{2,1,0:T(8,128)(2,1)S(1)} %get-tuple-element.51), channel_id=1, source_target_pairs={{3,0},{0,1},{1,2},{2,3},{7,4},{4,5},{5,6},{6,7},{11,8},{8,9},{9,10... | collective-permute-start | bytes 196616 | tf_op jit(solution)/shard_map/ppermute | solution.py:266
  119.6 6.3 %collective-permute-start.13 = (bf16[2,128,128]{2,1,0:T(8,128)(2,1)S(1)}, bf16[2,128,128]{2,1,0:T(8,128)(2,1)S(1)}, u32[]{:S(2)}, u32[]{:S(2)}) collective-permute-start(bf16[2,128,128]{2,1,0:T(8,128)(2,1)S(1)} %get-tuple-element.52), channel_id=1, source_target_pairs={{2,0},{3,1},{0,2},{1,3},{6,4},{7,5},{4,6},{5,7},{10,8},{11,9},{8,1... | collective-permute-start | bytes 196616 | tf_op jit(solution)/shard_map/ppermute | solution.py:266
  124.8 4.3 %collective-permute-start.14 = (bf16[2,128,128]{2,1,0:T(8,128)(2,1)S(1)}, bf16[2,128,128]{2,1,0:T(8,128)(2,1)S(1)}, u32[]{:S(2)}, u32[]{:S(2)}) collective-permute-start(bf16[2,128,128]{2,1,0:T(8,128)(2,1)S(1)} %get-tuple-element.53), channel_id=1, source_target_pairs={{1,0},{2,1},{3,2},{0,3},{5,4},{6,5},{7,6},{4,7},{9,8},{10,9},{11,1... | collective-permute-start | bytes 196616 | tf_op jit(solution)/shard_map/ppermute | solution.py:266
  136.7 7.3 %collective-permute-start.18 = (bf16[2,4,256,128]{3,2,1,0:T(8,128)(2,1)S(1)}, bf16[2,4,256,128]{3,2,1,0:T(8,128)(2,1)S(1)}, u32[]{:S(2)}, u32[]{:S(2)}) collective-permute-start(bf16[2,4,256,128]{3,2,1,0:T(8,128)(2,1)S(1)} %select_select_fusion.own_ref), channel_id=1, source_target_pairs={{8,0},{0,8},{9,1},{1,9},{10,2},{2,10},{11,3},{3,11},{12,4},{4,12},... | collective-permute-start | bytes 1572872 | tf_op jit(solution)/shard_map/ppermute | solution.py:266
  136.8 17.9 %all-to-all-start.4 = ((bf16[8,128,128]{2,1,0:T(8,128)(2,1)}), bf16[8,128,128]{2,1,0:T(8,128)(2,1)S(1)}, u32[]{:S(2)}, u32[]{:S(2)}) async-start(bf16[8,128,128]{2,1,0:T(8,128)(2,1)} %bitcast.24), calls=%async_computation.4 | async-start | bytes 524288 | tf_op jit(solution)/shard_map/all_to_all | solution.py:342
  (9 other events, 44.2 us)

commit v4 on v3

--- a/solution.py
+++ b/solution.py
@@ -330,17 +330,17 @@
     near = jnp.concatenate([half] + [shifted(half, "y", 4, by) for by in (1, 2, 3)], axis=0)
     far = shifted(near, "c", 2, 1)
     kv_all, q_rows, near, far, *got = lax.optimization_barrier((kv_all, q_rows, near, far, *got))
+
+    half = core_half(kv_all.reshape(4, 2, 4, 2 * BLOCK, HD), at_zl, at_c)
+    half, near, q_rows = lax.optimization_barrier((half, near, q_rows))
     q_all = lax.all_to_all(q_rows, EVERY, 0, 0, tiled=True)
-
-    half = core_half(kv_all.reshape(4, 2, 4, 2 * BLOCK, HD), at_zl, at_c)
-    half, near = lax.optimization_barrier((half, near))
     others = along_x(half)
     parts = attend_shared(pos, lists, five, got, near, far)
     shared = [parts[0]] + [shifted(parts[d], "y", 4, -d) for d in (1, 2, 3)]
     shared = ordered(y, shared, "order_views").reshape(PLANES, BLOCK, HD)
+    shared, *others = lax.optimization_barrier((shared, *others))
     shared, q_all = lax.optimization_barrier((shared, q_all))
     home = lax.all_to_all(shared, PLANE, 0, 0, tiled=True)
-    shared, q_all, *others = lax.optimization_barrier((shared, q_all, *others))
     own = true_half(others, at_x)
     other = shifted(own, "c", 2, 1)
     mixed = attend_main(pos, lists, q_all, kv_all, own, other)

time: 194 us -> 193 us (level)
    ppermute x19, waiting for transfers between devices: 42.4 us -> 45.2 us  [shifted(): return lax.ppermute(x, axis, [((i + by) % size, i) for i in range(size)])]
    all_to_all x1, waiting for transfers between devices: 2.55 us -> 0.01 us  [shards(): q_all = lax.all_to_all(q_rows, EVERY, 0, 0, tiled=True)]
    unnamed x23 -> x25, local copies, waits for them, and re-layouts: 5.64 us -> 5.64 us
  transfers between devices with their start and end apart: 23 -> 23, of which waited for: 19 -> 17; matrix products, arithmetic and copies ran while one was open for 1% -> 1% of each run, Pallas kernels for 9% -> 9%
where the time goes in v4:
time: 193 us
  waiting for transfers between devices  64 us (33%)
  starting transfers between devices  56.2 us (29%)
  blocking collectives  36.8 us (19%)
  Pallas kernels  22.7 us (12%)
  local copies, waits for them, and re-layouts  6.44 us (3%)
  between operations  3.71 us (2%)
  other arithmetic  2.83 us (1%)
    ppermute x19, waiting for transfers between devices, shifted(): return lax.ppermute(x, axis, [((i + by) % size, i) for i in range(size)])  45.2 us
    all_to_all x1, blocking collectives, shards(): main = lax.all_to_all(mixed, EVERY, 0, 0, tiled=True)  36.8 us
    ppermute x19, starting transfers between devices, shifted(): return lax.ppermute(x, axis, [((i + by) % size, i) for i in range(size)])  22.5 us
    all_to_all x1, waiting for transfers between devices, shards(): five = lax.all_to_all(five, PLANE, 0, 0, tiled=True)  15.9 us
    all_to_all x1, starting transfers between devices, shards(): q_all = lax.all_to_all(q_rows, EVERY, 0, 0, tiled=True)  10 us
    all_to_all x1, starting transfers between devices, shards(): five = lax.all_to_all(five, PLANE, 0, 0, tiled=True)  8.57 us
    all_to_all x1, starting transfers between devices, shards(): lax.all_to_all(kv_rows, EVERY, 0, 0, tiled=True).reshape(32, 2 * BLOCK, HD)  7.87 us
    pallas_call x1, Pallas kernels, attend_main(): pl.pallas_call(main_kernel, grid=(4,), in_specs=[SMEM, SMEM, blocks, ANY,...  7.41 us
  transfers between devices with their start and end apart: 23, of which 17 were waited for; matrix products, arithmetic and copies ran while one was open for 1% of the time, Pallas kernels for 9%

profile of v4, /device:TPU:32, one launch (start us, length us, event | category | flops | bytes accessed | tf_op | source)
XLA Modules:
  0.0 192.6 jit_solution(2233443849525084600)
XLA Ops:
  0.0 4.2 %shared_rows.1 = bf16[8,400,128]{2,1,0:T(8,128)(2,1)} custom-call(bf16[128,5120]{1,0:T(8,128)(2,1)} %q_ref.3, bf16[128,5120]{1,0:T(8,128)(2,1)} %k_ref.3, bf16[128,5120]{1,0:T(8,128)(2,1)} %v_ref.3, f32[1,5120]{1,0:T(1,128)} %bitcast.50, f32[1,5120]{1,0:T(1,128)} %bitcast.52, s32[1,8,8]{2,1,0:T(8,128)} %ids_ref.1, s32[1,8]{1,0:T(1,128)} %cnt_ref.1), custom_call_target="tpu_custom_call" | custom-call | tf_op jit(solution)/shard_map/shared_rows/pallas_call | solution.py:85
  4.2 8.6 %all-to-all-start = ((bf16[8,400,128]{2,1,0:T(8,128)(2,1)}), bf16[8,400,128]{2,1,0:T(8,128)(2,1)S(1)}, u32[]{:S(2)}, u32[]{:S(2)}) async-start(bf16[8,400,128]{2,1,0:T(8,128)(2,1)} %shared_rows.1), calls=%async_computation | async-start | bytes 1638400 | tf_op jit(solution)/shard_map/all_to_all | solution.py:316
  12.8 4.9 %own_rows.1 = (bf16[32,128,128]{2,1,0:T(8,128)(2,1)}, bf16[32,2,128,128]{3,2,1,0:T(8,128)(2,1)}) custom-call(bf16[128,5120]{1,0:T(8,128)(2,1)} %q_ref.3, bf16[128,5120]{1,0:T(8,128)(2,1)} %k_ref.3, bf16[128,5120]{1,0:T(8,128)(2,1)} %v_ref.3, f32[1,5120]{1,0:T(1,128)} %bitcast.51, f32[1,5120]{1,0:T(1,128)} %bitcast.53), custom_call_target="tpu_custom_call" | custom-call | tf_op jit(solution)/shard_map/own_rows/pallas_call | solution.py:94
  17.7 15.9 %all-to-all-done.five_ref = bf16[8,400,128]{2,1,0:T(8,128)(2,1)S(1)} async-done(((bf16[8,400,128]{2,1,0:T(8,128)(2,1)}), bf16[8,400,128]{2,1,0:T(8,128)(2,1)S(1)}, u32[]{:S(2)}, u32[]{:S(2)}) %all-to-all-start) | async-done | bytes 819232 | tf_op jit(solution)/shard_map/all_to_all | solution.py:316
  33.5 7.9 %all-to-all-start.1 = ((bf16[32,2,128,128]{3,2,1,0:T(8,128)(2,1)}), bf16[32,2,128,128]{3,2,1,0:T(8,128)(2,1)S(1)}, u32[]{:S(2)}, u32[]{:S(2)}) async-start(bf16[32,2,128,128]{3,2,1,0:T(8,128)(2,1)} %get-tuple-element.38), calls=%async_computation.1 | async-start | bytes 4194304 | tf_op jit(solution)/shard_map/all_to_all | solution.py:318
  47.1 2.8 %collective-permute-start.1 = (bf16[2,256,128]{2,1,0:T(8,128)(2,1)S(1)}, bf16[2,256,128]{2,1,0:T(8,128)(2,1)S(1)}, u32[]{:S(2)}, u32[]{:S(2)}) collective-permute-start(bf16[2,256,128]{2,1,0:T(8,128)(2,1)S(1)} %fusion.9), channel_id=1, source_target_pairs={{16,0},{32,16},{48,32},{0,48},{17,1},{33,17},{49,33},{1,49},{18,2}... | collective-permute-start | bytes 393224 | tf_op jit(solution)/shard_map/ppermute | solution.py:266
  51.8 2.8 %collective-permute-start.4 = (bf16[2,384,128]{2,1,0:T(8,128)(2,1)S(1)}, bf16[2,384,128]{2,1,0:T(8,128)(2,1)S(1)}, u32[]{:S(2)}, u32[]{:S(2)}) collective-permute-start(bf16[2,384,128]{2,1,0:T(8,128)(2,1)S(1)} %get-tuple-element.71), channel_id=1, source_target_pairs={{1,0},{2,1},{3,2},{0,3},{5,4},{6,5},{7,6},{4,7},{9,8},{10,9},{11,1... | collective-permute-start | bytes 589832 | tf_op jit(solution)/shard_map/ppermute | solution.py:266
  59.6 12.4 %collective-permute-done.4.rest_0_ = bf16[2,384,128]{2,1,0:T(8,128)(2,1)S(1)} collective-permute-done((bf16[2,384,128]{2,1,0:T(8,128)(2,1)S(1)}, bf16[2,384,128]{2,1,0:T(8,128)(2,1)S(1)}, u32[]{:S(2)}, u32[]{:S(2)}) %collective-permute-start.4) | collective-permute-done | bytes 196640 | tf_op jit(solution)/shard_map/ppermute | solution.py:266
  72.1 4.8 %collective-permute-done.6.rest_2_ = bf16[2,384,128]{2,1,0:T(8,128)(2,1)S(1)} collective-permute-done((bf16[2,384,128]{2,1,0:T(8,128)(2,1)S(1)}, bf16[2,384,128]{2,1,0:T(8,128)(2,1)S(1)}, u32[]{:S(2)}, u32[]{:S(2)}) %collective-permute-start.6) | collective-permute-done | bytes 196640 | tf_op jit(solution)/shard_map/ppermute | solution.py:266
  76.9 2.8 %collective-permute-start.7 = (bf16[2,256,128]{2,1,0:T(8,128)(2,1)S(1)}, bf16[2,256,128]{2,1,0:T(8,128)(2,1)S(1)}, u32[]{:S(2)}, u32[]{:S(2)}) collective-permute-start(bf16[2,256,128]{2,1,0:T(8,128)(2,1)S(1)} %select_select_fusion.1), channel_id=1, source_target_pairs={{1,0},{2,1},{3,2},{0,3},{5,4},{6,5},{7,6},{4,7},{9,8},{10,9},{11,1... | collective-permute-start | bytes 393224 | tf_op jit(solution)/shard_map/ppermute | solution.py:266
  80.7 5.6 %collective-permute-done.7 = bf16[2,256,128]{2,1,0:T(8,128)(2,1)S(1)} collective-permute-done((bf16[2,256,128]{2,1,0:T(8,128)(2,1)S(1)}, bf16[2,256,128]{2,1,0:T(8,128)(2,1)S(1)}, u32[]{:S(2)}, u32[]{:S(2)}) %collective-permute-start.7) | collective-permute-done | bytes 131104 | tf_op jit(solution)/shard_map/ppermute | solution.py:266
  89.7 1.9 collective-permute-done.10.rest_4_
  93.1 1.9 collective-permute-done.11
  96.0 10.0 %all-to-all-start.2 = ((bf16[32,128,128]{2,1,0:T(8,128)(2,1)}), bf16[32,128,128]{2,1,0:T(8,128)(2,1)}, u32[]{:S(2)}, u32[]{:S(2)}) async-start(bf16[32,128,128]{2,1,0:T(8,128)(2,1)} %get-tuple-element.58), calls=%async_computation.2 | async-start | bytes 2097152 | tf_op jit(solution)/shard_map/all_to_all | solution.py:336
  106.0 2.4 %collective-permute-start.15 = (bf16[2,4,256,128]{3,2,1,0:T(8,128)(2,1)}, bf16[2,4,256,128]{3,2,1,0:T(8,128)(2,1)}, u32[]{:S(2)}, u32[]{:S(2)}) collective-permute-start(bf16[2,4,256,128]{3,2,1,0:T(8,128)(2,1)} %fusion.4), channel_id=1, source_target_pairs={{16,0},{32,16},{48,32},{0,48},{17,1},{33,17},{49,33},{1,49},{18,2}... | collective-permute-start | bytes 1572872 | tf_op jit(solution)/shard_map/ppermute | solution.py:266
  114.3 3.7 %attend_shared.1 = (bf16[2,128,128]{2,1,0:T(8,128)(2,1)S(1)}, bf16[2,128,128]{2,1,0:T(8,128)(2,1)S(1)}, bf16[2,128,128]{2,1,0:T(8,128)(2,1)S(1)}, bf16[2,128,128]{2,1,0:T(8,128)(2,1)S(1)}) custom-call(s32[4]{0:T(128)S(1)} %pad_add_fusion.pos_ref, s32[4,8,9]{2,1,0:T(8,128)S(1)} %fusion.10.lists_ref, bf16[8,400,128]{2,1,0:T(8,128)(2,1)S(1)} %all-to-all-done.five_ref, ...), custom_call_target="tpu_custom_call" | custom-call | flops 536870912 | bytes 1572864 | tf_op jit(solution)/shard_map/attend_shared/pallas_call | solution.py:244
  119.6 2.7 %collective-permute-start.13 = (bf16[2,128,128]{2,1,0:T(8,128)(2,1)S(1)}, bf16[2,128,128]{2,1,0:T(8,128)(2,1)S(1)}, u32[]{:S(2)}, u32[]{:S(2)}) collective-permute-start(bf16[2,128,128]{2,1,0:T(8,128)(2,1)S(1)} %get-tuple-element.54), channel_id=1, source_target_pairs={{2,0},{3,1},{0,2},{1,3},{6,4},{7,5},{4,6},{5,7},{10,8},{11,9},{8,1... | collective-permute-start | bytes 196616 | tf_op jit(solution)/shard_map/ppermute | solution.py:266
  122.2 5.1 %collective-permute-done.12.rest_1_ = bf16[2,128,128]{2,1,0:T(8,128)(2,1)S(1)} collective-permute-done((bf16[2,128,128]{2,1,0:T(8,128)(2,1)S(1)}, bf16[2,128,128]{2,1,0:T(8,128)(2,1)S(1)}, u32[]{:S(2)}, u32[]{:S(2)}) %collective-permute-start.12) | collective-permute-done | bytes 65568 | tf_op jit(solution)/shard_map/ppermute | solution.py:266
  127.4 4.3 %collective-permute-done.14.rest_3_ = bf16[2,128,128]{2,1,0:T(8,128)(2,1)S(1)} collective-permute-done((bf16[2,128,128]{2,1,0:T(8,128)(2,1)S(1)}, bf16[2,128,128]{2,1,0:T(8,128)(2,1)S(1)}, u32[]{:S(2)}, u32[]{:S(2)}) %collective-permute-start.14) | collective-permute-done | bytes 65568 | tf_op jit(solution)/shard_map/ppermute | solution.py:266
  132.4 2.1 %collective-permute-done.17 = bf16[2,4,256,128]{3,2,1,0:T(8,128)(2,1)} collective-permute-done((bf16[2,4,256,128]{3,2,1,0:T(8,128)(2,1)}, bf16[2,4,256,128]{3,2,1,0:T(8,128)(2,1)}, u32[]{:S(2)}, u32[]{:S(2)}) %collective-permute-start.17) | collective-permute-done | bytes 524320 | tf_op jit(solution)/shard_map/ppermute | solution.py:266
  136.1 7.2 %all-to-all-start.4 = ((bf16[8,128,128]{2,1,0:T(8,128)(2,1)}), bf16[8,128,128]{2,1,0:T(8,128)(2,1)S(1)}, u32[]{:S(2)}, u32[]{:S(2)}) async-start(bf16[8,128,128]{2,1,0:T(8,128)(2,1)} %bitcast.24), calls=%async_computation.4 | async-start | bytes 524288 | tf_op jit(solution)/shard_map/all_to_all | solution.py:343
  143.4 7.4 %attend_main.1 = bf16[32,128,128]{2,1,0:T(8,128)(2,1)S(1)} custom-call(s32[4]{0:T(128)S(1)} %pad_add_fusion.pos_ref, s32[4,8,9]{2,1,0:T(8,128)S(1)} %fusion.10.lists_ref, bf16[32,128,128]{2,1,0:T(8,128)(2,1)} %all-to-all-done.2.q_ref, bf16[32,256,128]{2,1,0:T(8,128)(2,1)S(1)} %bitcast.49, bf16[2,4,256,128]{3,2,1,0:T(8,128)(2,1)S(1)} %select_select_fusion.own_ref, ...), custom_call_target="tpu_custom_call" | custom-call | flops 2147483648 | bytes 3145728 | tf_op jit(solution)/shard_map/attend_main/pallas_call | solution.py:194
  151.7 2.3 %all-to-all-done.4.five_ref = bf16[8,128,128]{2,1,0:T(8,128)(2,1)S(1)} async-done(((bf16[8,128,128]{2,1,0:T(8,128)(2,1)}), bf16[8,128,128]{2,1,0:T(8,128)(2,1)S(1)}, u32[]{:S(2)}, u32[]{:S(2)}) %all-to-all-start.4) | async-done | bytes 262176 | tf_op jit(solution)/shard_map/all_to_all | solution.py:343
  154.1 36.8 %all_to_all.25.main_ref = bf16[32,128,128]{2,1,0:T(8,128)(2,1)S(1)} all-to-all(bf16[32,128,128]{2,1,0:T(8,128)(2,1)} %copy-done), channel_id=1, replica_groups=mesh['zl'=4,'x'=4,'c'=2,'zh'=2,'y'=4] {'zl','zh','y'}, dimensions={0} | all-to-all | bytes 2097152 | tf_op jit(solution)/shard_map/all_to_all | solution.py:347
  (72 shorter events, 28.6 us)
Async XLA Ops:
  4.2 29.3 %all-to-all-start = ((bf16[8,400,128]{2,1,0:T(8,128)(2,1)}), bf16[8,400,128]{2,1,0:T(8,128)(2,1)S(1)}, u32[]{:S(2)}, u32[]{:S(2)}) async-start(bf16[8,400,128]{2,1,0:T(8,128)(2,1)} %shared_rows.1), calls=%async_computation | async-start | bytes 1638400 | tf_op jit(solution)/shard_map/all_to_all | solution.py:316
  33.5 59.4 %all-to-all-start.1 = ((bf16[32,2,128,128]{3,2,1,0:T(8,128)(2,1)}), bf16[32,2,128,128]{3,2,1,0:T(8,128)(2,1)S(1)}, u32[]{:S(2)}, u32[]{:S(2)}) async-start(bf16[32,2,128,128]{3,2,1,0:T(8,128)(2,1)} %get-tuple-element.38), calls=%async_computation.1 | async-start | bytes 4194304 | tf_op jit(solution)/shard_map/all_to_all | solution.py:318
  45.6 1.4 collective-permute-start
  47.1 8.7 %collective-permute-start.1 = (bf16[2,256,128]{2,1,0:T(8,128)(2,1)S(1)}, bf16[2,256,128]{2,1,0:T(8,128)(2,1)S(1)}, u32[]{:S(2)}, u32[]{:S(2)}) collective-permute-start(bf16[2,256,128]{2,1,0:T(8,128)(2,1)S(1)} %fusion.9), channel_id=1, source_target_pairs={{16,0},{32,16},{48,32},{0,48},{17,1},{33,17},{49,33},{1,49},{18,2}... | collective-permute-start | bytes 393224 | tf_op jit(solution)/shard_map/ppermute | solution.py:266
  50.0 7.9 %collective-permute-start.2 = (bf16[2,256,128]{2,1,0:T(8,128)(2,1)S(1)}, bf16[2,256,128]{2,1,0:T(8,128)(2,1)S(1)}, u32[]{:S(2)}, u32[]{:S(2)}) collective-permute-start(bf16[2,256,128]{2,1,0:T(8,128)(2,1)S(1)} %fusion.9), channel_id=1, source_target_pairs={{32,0},{48,16},{0,32},{16,48},{33,1},{49,17},{1,33},{17,49},{34,2}... | collective-permute-start | bytes 393224 | tf_op jit(solution)/shard_map/ppermute | solution.py:266
  50.8 8.8 %collective-permute-start.3 = (bf16[2,256,128]{2,1,0:T(8,128)(2,1)S(1)}, bf16[2,256,128]{2,1,0:T(8,128)(2,1)S(1)}, u32[]{:S(2)}, u32[]{:S(2)}) collective-permute-start(bf16[2,256,128]{2,1,0:T(8,128)(2,1)S(1)} %fusion.9), channel_id=1, source_target_pairs={{48,0},{0,16},{16,32},{32,48},{49,1},{1,17},{17,33},{33,49},{50,2}... | collective-permute-start | bytes 393224 | tf_op jit(solution)/shard_map/ppermute | solution.py:266
  51.8 20.3 %collective-permute-start.4 = (bf16[2,384,128]{2,1,0:T(8,128)(2,1)S(1)}, bf16[2,384,128]{2,1,0:T(8,128)(2,1)S(1)}, u32[]{:S(2)}, u32[]{:S(2)}) collective-permute-start(bf16[2,384,128]{2,1,0:T(8,128)(2,1)S(1)} %get-tuple-element.71), channel_id=1, source_target_pairs={{1,0},{2,1},{3,2},{0,3},{5,4},{6,5},{7,6},{4,7},{9,8},{10,9},{11,1... | collective-permute-start | bytes 589832 | tf_op jit(solution)/shard_map/ppermute | solution.py:266
  54.5 17.5 %collective-permute-start.5 = (bf16[2,384,128]{2,1,0:T(8,128)(2,1)S(1)}, bf16[2,384,128]{2,1,0:T(8,128)(2,1)S(1)}, u32[]{:S(2)}, u32[]{:S(2)}) collective-permute-start(bf16[2,384,128]{2,1,0:T(8,128)(2,1)S(1)} %get-tuple-element.70), channel_id=1, source_target_pairs={{2,0},{3,1},{0,2},{1,3},{6,4},{7,5},{4,6},{5,7},{10,8},{11,9},{8,1... | collective-permute-start | bytes 589832 | tf_op jit(solution)/shard_map/ppermute | solution.py:266
  55.9 21.0 %collective-permute-start.6 = (bf16[2,384,128]{2,1,0:T(8,128)(2,1)S(1)}, bf16[2,384,128]{2,1,0:T(8,128)(2,1)S(1)}, u32[]{:S(2)}, u32[]{:S(2)}) collective-permute-start(bf16[2,384,128]{2,1,0:T(8,128)(2,1)S(1)} %get-tuple-element.69), channel_id=1, source_target_pairs={{3,0},{0,1},{1,2},{2,3},{7,4},{4,5},{5,6},{6,7},{11,8},{8,9},{9,10... | collective-permute-start | bytes 589832 | tf_op jit(solution)/shard_map/ppermute | solution.py:266
  76.9 9.5 %collective-permute-start.7 = (bf16[2,256,128]{2,1,0:T(8,128)(2,1)S(1)}, bf16[2,256,128]{2,1,0:T(8,128)(2,1)S(1)}, u32[]{:S(2)}, u32[]{:S(2)}) collective-permute-start(bf16[2,256,128]{2,1,0:T(8,128)(2,1)S(1)} %select_select_fusion.1), channel_id=1, source_target_pairs={{1,0},{2,1},{3,2},{0,3},{5,4},{6,5},{7,6},{4,7},{9,8},{10,9},{11,1... | collective-permute-start | bytes 393224 | tf_op jit(solution)/shard_map/ppermute | solution.py:266
  79.7 8.2 %collective-permute-start.8 = (bf16[2,256,128]{2,1,0:T(8,128)(2,1)S(1)}, bf16[2,256,128]{2,1,0:T(8,128)(2,1)S(1)}, u32[]{:S(2)}, u32[]{:S(2)}) collective-permute-start(bf16[2,256,128]{2,1,0:T(8,128)(2,1)S(1)} %select_select_fusion.1), channel_id=1, source_target_pairs={{2,0},{3,1},{0,2},{1,3},{6,4},{7,5},{4,6},{5,7},{10,8},{11,9},{8,1... | collective-permute-start | bytes 393224 | tf_op jit(solution)/shard_map/ppermute | solution.py:266
  79.7 9.8 %collective-permute-start.9 = (bf16[2,256,128]{2,1,0:T(8,128)(2,1)S(1)}, bf16[2,256,128]{2,1,0:T(8,128)(2,1)S(1)}, u32[]{:S(2)}, u32[]{:S(2)}) collective-permute-start(bf16[2,256,128]{2,1,0:T(8,128)(2,1)S(1)} %select_select_fusion.1), channel_id=1, source_target_pairs={{3,0},{0,1},{1,2},{2,3},{7,4},{4,5},{5,6},{6,7},{11,8},{8,9},{9,10... | collective-permute-start | bytes 393224 | tf_op jit(solution)/shard_map/ppermute | solution.py:266
  89.5 2.0 %collective-permute-start.10 = (bf16[8,256,128]{2,1,0:T(8,128)(2,1)S(1)}, bf16[8,256,128]{2,1,0:T(8,128)(2,1)S(1)}, u32[]{:S(2)}, u32[]{:S(2)}) collective-permute-start(bf16[8,256,128]{2,1,0:T(8,128)(2,1)S(1)} %constant_dynamic-update-slice_fusion.rest_3_), channel_id=1, source_target_pairs={{8,0},{0,8},{9,1},{1,9},{10,2},{2,10},{11,3},{3,11},{12,4},{4,12},... | collective-permute-start | bytes 1572872 | tf_op jit(solution)/shard_map/ppermute | solution.py:266
  93.0 2.0 %collective-permute-start.11 = (bf16[2,4,256,128]{3,2,1,0:T(8,128)(2,1)S(1)}, bf16[2,4,256,128]{3,2,1,0:T(8,128)(2,1)S(1)}, u32[]{:S(2)}, u32[]{:S(2)}) collective-permute-start(bf16[2,4,256,128]{3,2,1,0:T(8,128)(2,1)S(1)} %fusion.1), channel_id=1, source_target_pairs={{8,0},{0,8},{9,1},{1,9},{10,2},{2,10},{11,3},{3,11},{12,4},{4,12},... | collective-permute-start | bytes 1572872 | tf_op jit(solution)/shard_map/ppermute | solution.py:266
  96.0 40.2 %all-to-all-start.2 = ((bf16[32,128,128]{2,1,0:T(8,128)(2,1)}), bf16[32,128,128]{2,1,0:T(8,128)(2,1)}, u32[]{:S(2)}, u32[]{:S(2)}) async-start(bf16[32,128,128]{2,1,0:T(8,128)(2,1)} %get-tuple-element.58), calls=%async_computation.2 | async-start | bytes 2097152 | tf_op jit(solution)/shard_map/all_to_all | solution.py:336
  106.0 26.4 %collective-permute-start.15 = (bf16[2,4,256,128]{3,2,1,0:T(8,128)(2,1)}, bf16[2,4,256,128]{3,2,1,0:T(8,128)(2,1)}, u32[]{:S(2)}, u32[]{:S(2)}) collective-permute-start(bf16[2,4,256,128]{3,2,1,0:T(8,128)(2,1)} %fusion.4), channel_id=1, source_target_pairs={{16,0},{32,16},{48,32},{0,48},{17,1},{33,17},{49,33},{1,49},{18,2}... | collective-permute-start | bytes 1572872 | tf_op jit(solution)/shard_map/ppermute | solution.py:266
  108.3 24.0 %collective-permute-start.16 = (bf16[2,4,256,128]{3,2,1,0:T(8,128)(2,1)}, bf16[2,4,256,128]{3,2,1,0:T(8,128)(2,1)}, u32[]{:S(2)}, u32[]{:S(2)}) collective-permute-start(bf16[2,4,256,128]{3,2,1,0:T(8,128)(2,1)} %fusion.4), channel_id=1, source_target_pairs={{32,0},{48,16},{0,32},{16,48},{33,1},{49,17},{1,33},{17,49},{34,2}... | collective-permute-start | bytes 1572872 | tf_op jit(solution)/shard_map/ppermute | solution.py:266
  109.9 24.6 %collective-permute-start.17 = (bf16[2,4,256,128]{3,2,1,0:T(8,128)(2,1)}, bf16[2,4,256,128]{3,2,1,0:T(8,128)(2,1)}, u32[]{:S(2)}, u32[]{:S(2)}) collective-permute-start(bf16[2,4,256,128]{3,2,1,0:T(8,128)(2,1)} %fusion.4), channel_id=1, source_target_pairs={{48,0},{0,16},{16,32},{32,48},{49,1},{1,17},{17,33},{33,49},{50,2}... | collective-permute-start | bytes 1572872 | tf_op jit(solution)/shard_map/ppermute | solution.py:266
  114.3 20.2 %copy-start.9 = (bf16[2,4,256,128]{3,2,1,0:T(8,128)(2,1)S(1)}, bf16[2,4,256,128]{3,2,1,0:T(8,128)(2,1)}, u32[]{:S(2)}) copy-start(bf16[2,4,256,128]{3,2,1,0:T(8,128)(2,1)} %fusion.4) | copy-start | bytes 1572868
  118.0 9.3 %collective-permute-start.12 = (bf16[2,128,128]{2,1,0:T(8,128)(2,1)S(1)}, bf16[2,128,128]{2,1,0:T(8,128)(2,1)S(1)}, u32[]{:S(2)}, u32[]{:S(2)}) collective-permute-start(bf16[2,128,128]{2,1,0:T(8,128)(2,1)S(1)} %get-tuple-element.53), channel_id=1, source_target_pairs={{3,0},{0,1},{1,2},{2,3},{7,4},{4,5},{5,6},{6,7},{11,8},{8,9},{9,10... | collective-permute-start | bytes 196616 | tf_op jit(solution)/shard_map/ppermute | solution.py:266
  119.6 7.8 %collective-permute-start.13 = (bf16[2,128,128]{2,1,0:T(8,128)(2,1)S(1)}, bf16[2,128,128]{2,1,0:T(8,128)(2,1)S(1)}, u32[]{:S(2)}, u32[]{:S(2)}) collective-permute-start(bf16[2,128,128]{2,1,0:T(8,128)(2,1)S(1)} %get-tuple-element.54), channel_id=1, source_target_pairs={{2,0},{3,1},{0,2},{1,3},{6,4},{7,5},{4,6},{5,7},{10,8},{11,9},{8,1... | collective-permute-start | bytes 196616 | tf_op jit(solution)/shard_map/ppermute | solution.py:266
  127.4 4.3 %collective-permute-start.14 = (bf16[2,128,128]{2,1,0:T(8,128)(2,1)S(1)}, bf16[2,128,128]{2,1,0:T(8,128)(2,1)S(1)}, u32[]{:S(2)}, u32[]{:S(2)}) collective-permute-start(bf16[2,128,128]{2,1,0:T(8,128)(2,1)S(1)} %get-tuple-element.55), channel_id=1, source_target_pairs={{1,0},{2,1},{3,2},{0,3},{5,4},{6,5},{7,6},{4,7},{9,8},{10,9},{11,1... | collective-permute-start | bytes 196616 | tf_op jit(solution)/shard_map/ppermute | solution.py:266
  136.0 7.3 %collective-permute-start.18 = (bf16[2,4,256,128]{3,2,1,0:T(8,128)(2,1)S(1)}, bf16[2,4,256,128]{3,2,1,0:T(8,128)(2,1)S(1)}, u32[]{:S(2)}, u32[]{:S(2)}) collective-permute-start(bf16[2,4,256,128]{3,2,1,0:T(8,128)(2,1)S(1)} %select_select_fusion.own_ref), channel_id=1, source_target_pairs={{8,0},{0,8},{9,1},{1,9},{10,2},{2,10},{11,3},{3,11},{12,4},{4,12},... | collective-permute-start | bytes 1572872 | tf_op jit(solution)/shard_map/ppermute | solution.py:266
  136.1 17.9 %all-to-all-start.4 = ((bf16[8,128,128]{2,1,0:T(8,128)(2,1)}), bf16[8,128,128]{2,1,0:T(8,128)(2,1)S(1)}, u32[]{:S(2)}, u32[]{:S(2)}) async-start(bf16[8,128,128]{2,1,0:T(8,128)(2,1)} %bitcast.24), calls=%async_computation.4 | async-start | bytes 524288 | tf_op jit(solution)/shard_map/all_to_all | solution.py:343
  (10 other events, 61.5 us)
